TPU v7x, 128 devices: a whole 4x4x4 slice. The times are simulated.
128 devices in a mesh: cp: 8 (over z, x_lo), ep: 16 (over x_hi, y, core).
Axes of the slice: x: 4 (x_hi: 2, x_lo: 2; x = x_hi * 2 + x_lo), y: 4, z: 4, core: 2. Of those that a mesh axis runs over, the one named last changes fastest.
Arguments:
- resid: bfloat16 [16, 1024, 2048], P('ep', 'cp'), may hold values from -6 to 6
- query: bfloat16 [16, 1024, 4096], P('ep', 'cp'), may hold values from -100 to 100
- keys: bfloat16 [16, 1024, 512], P('ep', 'cp'), may hold values from -4.5 to 4.5
- values: bfloat16 [16, 1024, 512], P('ep', 'cp'), may hold values from -6 to 6
- out_proj: bfloat16 [4096, 2048], P('cp'), may hold values from -0.09375 to 0.09375
- norm_gain: float32 [2048], replicated, may hold values from 0.4 to 2.5
- expert_ids: int32 [16, 1024, 8], P('ep', 'cp'), may hold values from 0 to 127, all different within a row; in each aligned block of 128 rows (0 to 127, 128 to 255, ..., all dimensions but the last counted through in order) at most 10 rows name the same one
- route_gates: float32 [16, 1024, 8], P('ep', 'cp'), may hold values from 0.05 to 0.3
- w_gate: bfloat16 [128, 2048, 768], P(('cp', 'ep')), may hold values from -0.125 to 0.125
- w_up: bfloat16 [128, 2048, 768], P(('cp', 'ep')), may hold values from -0.125 to 0.125
- w_down: bfloat16 [128, 768, 2048], P(('cp', 'ep')), may hold values from -0.21875 to 0.21875
- cotangent: bfloat16 [16, 1024, 2048], P('ep', 'cp'), may hold values from -6 to 6
Outputs:
- layer_out: bfloat16 [16, 1024, 2048], P('ep', 'cp')
- grad_hidden: float32 [16, 1024, 2048], P('ep', 'cp')
Inputs may be any that keep to these rules, and one draw needn't show every extreme that they name: `expert_ids`: each token names 8 different experts; among the 128 tokens of one device (aligned blocks of 128 consecutive positions of a sequence) no expert is named more than 10 times, a bound that some block reaches.
All inputs are finite; a program needn't handle non-finite values.
Results may differ from a plain program's by a relative error of at most 0.015.
Values may be sent and summed in bfloat16 or wider, within the bound.
A program may use at most 192 MiB of HBM per device.

v0:
```python
import jax
import jax.numpy as jnp
from jax import lax
from jax.sharding import PartitionSpec as P

QHEADS = 32
KVHEADS = 4
HEAD = 128
TOPK = 8


EPSILON = 1e-06


def norm_rows(hidden_rows, gain):
    mean_square = jnp.mean(hidden_rows * hidden_rows, axis=-1, keepdims=True)
    return hidden_rows * lax.rsqrt(mean_square + EPSILON) * gain


def silu_parts(gate_pre):
    sigmoid_value = jax.nn.sigmoid(gate_pre)
    return (gate_pre * sigmoid_value, sigmoid_value * (1.0 + gate_pre * (1.0 - sigmoid_value)))


def to_owners(buffer):
    moved = lax.all_to_all(buffer, ("cp", "ep"), split_axis=0, concat_axis=0, tiled=True)
    return moved


def on_device(
    resid,
    query,
    keys,
    values,
    out_proj,
    norm_gain,
    expert_ids,
    route_gates,
    w_gate,
    w_up,
    w_down,
    cotangent,
):
    cp_count = lax.axis_size("cp")
    ep_count = lax.axis_size("ep")
    tok_rows = resid.shape[1]
    model_width = resid.shape[2]
    seq_rows = tok_rows * cp_count
    kv_repeat = max(cp_count // KVHEADS, 1)

    def widen(source):
        split_heads = source[0].reshape(tok_rows, KVHEADS, HEAD)
        return jnp.repeat(split_heads, kv_repeat, axis=1).reshape(
            tok_rows, KVHEADS * kv_repeat * HEAD
        )

    head_query, head_keys, head_values = (
        lax.all_to_all(query[0], "cp", split_axis=1, concat_axis=0, tiled=True),
        lax.all_to_all(widen(keys), "cp", split_axis=1, concat_axis=0, tiled=True),
        lax.all_to_all(widen(values), "cp", split_axis=1, concat_axis=0, tiled=True),
    )
    local_heads = QHEADS // cp_count
    local_kv = KVHEADS * kv_repeat // cp_count
    per_group = local_heads // local_kv
    grouped_query = head_query.reshape(seq_rows, local_kv, per_group, HEAD)
    grouped_keys = head_keys.reshape(seq_rows, local_kv, HEAD)
    grouped_values = head_values.reshape(seq_rows, local_kv, HEAD)
    scores = jnp.einsum(
        "qagd,kad->agqk", grouped_query, grouped_keys, preferred_element_type=jnp.float32
    ) * HEAD ** (-0.5)
    causal = lax.broadcasted_iota(jnp.int32, (seq_rows, seq_rows), 0) >= lax.broadcasted_iota(
        jnp.int32, (seq_rows, seq_rows), 1
    )
    scores = jnp.where(causal[None, None], scores, -jnp.inf)
    highest = jnp.max(scores, axis=-1, keepdims=True)
    weights = jnp.exp(scores - highest)
    probs = (weights / jnp.sum(weights, axis=-1, keepdims=True)).astype(jnp.bfloat16)
    attended = jnp.einsum(
        "agqk,kad->qagd", probs, grouped_values, preferred_element_type=jnp.float32
    )
    attn_out = attended.reshape(seq_rows, local_heads * HEAD).astype(jnp.bfloat16)
    attn_proj = lax.psum_scatter(
        jnp.dot(attn_out, out_proj, preferred_element_type=jnp.float32).astype(jnp.bfloat16),
        "cp",
        scatter_dimension=0,
        tiled=True,
    ).astype(jnp.float32)
    hidden = resid[0].astype(jnp.float32) + attn_proj
    normed_full, pullback = jax.vjp(lambda hidden_rows: norm_rows(hidden_rows, norm_gain), hidden)
    normed = normed_full.astype(jnp.bfloat16)
    flat_ids = expert_ids[0].reshape(-1)
    flat_gates = route_gates[0].reshape(-1)
    total_rows = flat_ids.shape[0]
    expert_count = cp_count * ep_count
    capacity = tok_rows * TOPK * 5 // (4 * expert_count)
    onehot = (flat_ids[:, None] == jnp.arange(expert_count, dtype=jnp.int32)[None, :]).astype(
        jnp.int32
    )
    ranks = jnp.sum(jnp.cumsum(onehot, axis=0) * onehot, axis=1) - 1
    slot_index = flat_ids * capacity + ranks
    slot_source = jnp.full((expert_count * capacity,), total_rows, jnp.int32)
    slot_source = slot_source.at[slot_index].set(jnp.arange(total_rows, dtype=jnp.int32))
    filled = slot_source < total_rows
    slot_clamped = jnp.minimum(slot_source, total_rows - 1)
    slot_token = slot_clamped // TOPK
    dispatch = jnp.where(filled[:, None], normed[slot_token], jnp.zeros((), jnp.bfloat16))
    dispatch = dispatch.reshape(expert_count, capacity, model_width)
    gate_weight = w_gate[0]
    up_weight = w_up[0]
    down_weight = w_down[0]
    arrived = to_owners(dispatch).reshape(expert_count * capacity, model_width)
    gate_pre = jnp.dot(arrived, gate_weight, preferred_element_type=jnp.float32)
    up_pre = jnp.dot(arrived, up_weight, preferred_element_type=jnp.float32)
    silu_value, silu_slope = silu_parts(gate_pre)
    inner = (silu_value * up_pre).astype(jnp.bfloat16)
    expert_out = jnp.dot(inner, down_weight, preferred_element_type=jnp.float32).astype(
        jnp.bfloat16
    )
    returned = to_owners(expert_out.reshape(expert_count, capacity, model_width))
    returned = returned.reshape(expert_count * capacity, model_width)
    picked = returned[slot_index].astype(jnp.float32).reshape(tok_rows, TOPK, model_width)
    moe_sum = jnp.sum(picked * flat_gates.reshape(tok_rows, TOPK, 1), axis=1)
    layer_out = (hidden + moe_sum).astype(jnp.bfloat16)
    cot_rows = cotangent[0]
    grad_slots = flat_gates[slot_clamped][:, None] * cot_rows[slot_token].astype(jnp.float32)
    grad_slots = jnp.where(filled[:, None], grad_slots, 0.0).astype(jnp.bfloat16)
    grad_arrived = to_owners(grad_slots.reshape(expert_count, capacity, model_width))
    grad_arrived = grad_arrived.reshape(expert_count * capacity, model_width)
    contract_last = (((1,), (1,)), ((), ()))
    grad_inner = lax.dot_general(
        grad_arrived, down_weight, contract_last, preferred_element_type=jnp.float32
    )
    grad_gate = (grad_inner * up_pre * silu_slope).astype(jnp.bfloat16)
    grad_up = (grad_inner * silu_value).astype(jnp.bfloat16)
    grad_input = lax.dot_general(
        grad_gate, gate_weight, contract_last, preferred_element_type=jnp.float32
    )
    grad_input = grad_input + lax.dot_general(
        grad_up, up_weight, contract_last, preferred_element_type=jnp.float32
    )
    grad_input = grad_input.astype(jnp.bfloat16).reshape(expert_count, capacity, model_width)
    grad_back = to_owners(grad_input).reshape(expert_count * capacity, model_width)
    normed_grad = jnp.sum(
        grad_back[slot_index].astype(jnp.float32).reshape(tok_rows, TOPK, model_width), axis=1
    )
    grad_hidden = cot_rows.astype(jnp.float32) + pullback(normed_grad)[0]
    return (layer_out[None], grad_hidden[None])


def solution(mesh):
    placed = (
        P("ep", "cp", None),
        P("ep", "cp", None),
        P("ep", "cp", None),
        P("ep", "cp", None),
        P("cp", None),
        P(),
        P("ep", "cp", None),
        P("ep", "cp", None),
        P(("cp", "ep"), None, None),
        P(("cp", "ep"), None, None),
        P(("cp", "ep"), None, None),
        P("ep", "cp", None),
    )
    return jax.shard_map(
        on_device,
        mesh=mesh,
        in_specs=placed,
        out_specs=(P("ep", "cp", None), P("ep", "cp", None)),
        check_vma=False,
    )
```

profile of v0, /device:TPU:40, one launch (start us, length us, event | category | flops | bytes accessed | tf_op | source)
XLA Modules:
  0.0 695.1 jit_solution(275623500422775168)
XLA Ops:
  9.1 6.3 all-to-all-start.2
  21.2 5.7 all-to-all-start.1
  28.5 11.1 %all-to-all-done.1 = bf16[128,8,512]{0,2,1:T(8,128)(2,1)} async-done(((bf16[128,8,512]{0,2,1:T(8,128)(2,1)}), bf16[128,8,512]{0,2,1:T(8,128)(2,1)}, u32[]{:S(2)}, u32[]{:S(2)}) %all-to-all-start.1) | async-done | bytes 1048608 | tf_op jit(solution)/shard_map/all_to_all | solution.py:58
  82.4 82.7 %reduce-scatter.2.cloned.1.call-done = bf16[128,2048]{1,0:T(8,128)(2,1)} async-done(((bf16[1024,2048]{1,0:T(8,128)(2,1)}), bf16[128,2048]{1,0:T(8,128)(2,1)}) %reduce-scatter.2.cloned.1.call-update) | async-done | bytes 524304 | tf_op jit(solution)/shard_map/reduce_scatter | solution.py:82
  169.3 11.9 %gather_fusion = bf16[1280,2048]{1,0:T(8,128)(2,1)} fusion(bf16[128,2048]{1,0:T(8,128)(2,1)} %multiply_convert_fusion.6, s32[2048]{0:T(1024)S(1)} %pad_clamp_fusion.1), kind=kCustom, calls=%fused_computation | custom fusion | bytes 10490880 | tf_op jit(solution)/shard_map/gather | solution.py:106
  181.3 9.6 %gather.18 = bf16[128,10,2048]{2,1,0:T(8,128)(2,1)} reshape(bf16[1280,2048]{1,0:T(8,128)(2,1)} %gather_fusion) | data formatting | bytes 10485760 | tf_op jit(solution)/shard_map/gather | solution.py:106
  190.8 7.4 %broadcast_select_fusion = bf16[128,10,2048]{2,1,0:T(8,128)(2,1)} fusion(bf16[128,10,2048]{2,1,0:T(8,128)(2,1)} %gather.18, pred[128,10]{1,0:T(8,128)(4,1)S(1)} %broadcast_in_dim.74), kind=kLoop, calls=%fused_computation.18 | loop fusion | flops 2621440 | bytes 10487040 | tf_op jit(solution)/shard_map/jit(_where)/select_n | solution.py:106
  198.2 9.7 %all-to-all-start.3 = ((bf16[128,10,2048]{2,1,0:T(8,128)(2,1)}), bf16[128,10,2048]{2,1,0:T(8,128)(2,1)}, u32[]{:S(2)}, u32[]{:S(2)}) async-start(bf16[128,10,2048]{2,1,0:T(8,128)(2,1)} %broadcast_select_fusion), calls=%async_computation.4 | async-start | bytes 16777216 | tf_op jit(solution)/shard_map/all_to_all | solution.py:26
  213.3 12.0 %gather_fusion.3 = bf16[1280,2048]{1,0:T(8,128)(2,1)} fusion(bf16[128,2048]{1,0:T(8,128)(2,1)} %bitcast.96, s32[2048]{0:T(1024)S(1)} %pad_clamp_fusion.1), kind=kCustom, calls=%fused_computation.3 | custom fusion | bytes 10490880 | tf_op jit(solution)/shard_map/gather | solution.py:125
  225.3 10.3 %reshape.194 = f32[128,10,2048]{2,1,0:T(8,128)} reshape(bf16[1280,2048]{1,0:T(8,128)(2,1)} %gather_fusion.3) | data formatting | bytes 15728640 | tf_op jit(solution)/shard_map/convert_element_type | solution.py:125
  235.6 9.2 %select_convert_fusion = bf16[128,10,2048]{2,1,0:T(8,128)(2,1)} fusion(f32[128,10,2048]{2,1,0:T(8,128)} %reshape.194, f32[128,10]{1,0:T(8,128)S(1)} %mul.144, pred[128,10]{1,0:T(8,128)(4,1)S(1)} %broadcast_in_dim.74), kind=kLoop, calls=%fused_computation.7 | loop fusion | flops 7864320 | bytes 15735040 | tf_op jit(solution)/shard_map/convert_element_type | solution.py:126
  244.9 68.6 %all-to-all-done.3 = bf16[128,10,2048]{2,1,0:T(8,128)(2,1)} async-done(((bf16[128,10,2048]{2,1,0:T(8,128)(2,1)}), bf16[128,10,2048]{2,1,0:T(8,128)(2,1)}, u32[]{:S(2)}, u32[]{:S(2)}) %all-to-all-start.3) | async-done | bytes 5242912 | tf_op jit(solution)/shard_map/all_to_all | solution.py:26
  313.4 9.0 %all-to-all-start.5 = ((bf16[128,10,2048]{2,1,0:T(8,128)(2,1)}), bf16[128,10,2048]{2,1,0:T(8,128)(2,1)}, u32[]{:S(2)}, u32[]{:S(2)}) async-start(bf16[128,10,2048]{2,1,0:T(8,128)(2,1)} %select_convert_fusion), calls=%async_computation.6 | async-start | bytes 16777216 | tf_op jit(solution)/shard_map/all_to_all | solution.py:26
  322.4 9.8 %reshape.186 = bf16[1280,2048]{1,0:T(8,128)(2,1)} reshape(bf16[128,10,2048]{2,1,0:T(8,128)(2,1)} %all-to-all-done.3) | data formatting | bytes 10485760 | tf_op jit(solution)/shard_map/reshape | solution.py:111
  332.3 7.2 %fusion.14 = f32[1280,768]{1,0:T(8,128)S(1)} fusion(bf16[1280,2048]{1,0:T(8,128)(2,1)} %reshape.186, bf16[1,2048,768]{2,1,0:T(8,128)(2,1)} %param.20), kind=kOutput, calls=%fused_computation.35 | convolution fusion | flops 4026531840 | bytes 12320768 | tf_op jit(solution)/shard_map/dot_general | solution.py:112
  345.8 6.1 convolution_convert_fusion
  351.8 9.6 %reshape.187 = bf16[128,10,2048]{2,1,0:T(8,128)(2,1)} reshape(bf16[1280,2048]{1,0:T(8,128)(2,1)} %convolution_convert_fusion) | data formatting | bytes 10485760 | tf_op jit(solution)/shard_map/reshape | solution.py:119
  361.4 66.3 %all-to-all-done.5 = bf16[128,10,2048]{2,1,0:T(8,128)(2,1)} async-done(((bf16[128,10,2048]{2,1,0:T(8,128)(2,1)}), bf16[128,10,2048]{2,1,0:T(8,128)(2,1)}, u32[]{:S(2)}, u32[]{:S(2)}) %all-to-all-start.5) | async-done | bytes 5242912 | tf_op jit(solution)/shard_map/all_to_all | solution.py:26
  427.8 8.4 %all-to-all-start.4 = ((bf16[128,10,2048]{2,1,0:T(8,128)(2,1)}), bf16[128,10,2048]{2,1,0:T(8,128)(2,1)}, u32[]{:S(2)}, u32[]{:S(2)}) async-start(bf16[128,10,2048]{2,1,0:T(8,128)(2,1)} %reshape.187), calls=%async_computation.5 | async-start | bytes 16777216 | tf_op jit(solution)/shard_map/all_to_all | solution.py:26
  436.2 9.9 %reshape.189 = bf16[1280,2048]{1,0:T(8,128)(2,1)} reshape(bf16[128,10,2048]{2,1,0:T(8,128)(2,1)} %all-to-all-done.5) | data formatting | bytes 10485760 | tf_op jit(solution)/shard_map/reshape | solution.py:128
  446.1 6.4 fusion.6
  454.5 8.0 %fusion.12 = f32[1280,2048]{1,0:T(8,128)} fusion(bf16[1,2048,768]{2,1,0:T(8,128)(2,1)S(1)} %copy-done.18, f32[1280,768]{1,0:T(8,128)S(1)} %copy-done.23, f32[1280,768]{1,0:T(8,128)S(1)} %fusion.6, f32[1280,768]{1,0:T(8,128)S(1)} %copy-done.26), kind=kOutput, calls=%fused_computation.33 | convolution fusion | flops 4036362240 | bytes 25427968 | tf_op jit(solution)/shard_map/dot_general | solution.py:135
  462.6 10.2 %add_convert_fusion = bf16[1280,2048]{1,0:T(8,128)(2,1)} fusion(f32[1280,2048]{1,0:T(8,128)} %fusion.12, bf16[1,2048,768]{2,1,0:T(8,128)(2,1)S(1)} %copy-done.20, f32[1280,768]{1,0:T(8,128)} %copy-done.24, f32[1280,768]{1,0:T(8,128)S(1)} %copy-done.23), kind=kOutput, calls=%fused_computation.12 | convolution fusion | flops 4037672960 | bytes 26738688 | tf_op jit(solution)/shard_map/dot_general | solution.py:138
  472.8 9.6 %reshape.190 = bf16[128,10,2048]{2,1,0:T(8,128)(2,1)} reshape(bf16[1280,2048]{1,0:T(8,128)(2,1)} %add_convert_fusion) | data formatting | bytes 10485760 | tf_op jit(solution)/shard_map/reshape | solution.py:141
  482.3 59.3 %all-to-all-done.4 = bf16[128,10,2048]{2,1,0:T(8,128)(2,1)} async-done(((bf16[128,10,2048]{2,1,0:T(8,128)(2,1)}), bf16[128,10,2048]{2,1,0:T(8,128)(2,1)}, u32[]{:S(2)}, u32[]{:S(2)}) %all-to-all-start.4) | async-done | bytes 5242912 | tf_op jit(solution)/shard_map/all_to_all | solution.py:26
  541.6 8.5 %all-to-all-start.6 = ((bf16[128,10,2048]{2,1,0:T(8,128)(2,1)}), bf16[128,10,2048]{2,1,0:T(8,128)(2,1)}, u32[]{:S(2)}, u32[]{:S(2)}) async-start(bf16[128,10,2048]{2,1,0:T(8,128)(2,1)} %reshape.190), calls=%async_computation.7 | async-start | bytes 16777216 | tf_op jit(solution)/shard_map/all_to_all | solution.py:26
  550.2 9.9 %reshape.188 = bf16[1280,2048]{1,0:T(8,128)(2,1)} reshape(bf16[128,10,2048]{2,1,0:T(8,128)(2,1)} %all-to-all-done.4) | data formatting | bytes 10485760 | tf_op jit(solution)/shard_map/reshape | solution.py:120
  560.0 12.0 %gather_fusion.1 = bf16[1024,2048]{1,0:T(8,128)(2,1)} fusion(bf16[1280,2048]{1,0:T(8,128)(2,1)} %reshape.188, s32[1024]{0:T(1024)S(1)} %broadcast_clamp_fusion), kind=kCustom, calls=%fused_computation.1 | custom fusion | bytes 8392704 | tf_op jit(solution)/shard_map/gather | solution.py:121
  572.0 83.4 %all-to-all-done.6 = bf16[128,10,2048]{2,1,0:T(8,128)(2,1)} async-done(((bf16[128,10,2048]{2,1,0:T(8,128)(2,1)}), bf16[128,10,2048]{2,1,0:T(8,128)(2,1)}, u32[]{:S(2)}, u32[]{:S(2)}) %all-to-all-start.6) | async-done | bytes 5242912 | tf_op jit(solution)/shard_map/all_to_all | solution.py:26
  655.4 9.8 %reshape.191 = bf16[1280,2048]{1,0:T(8,128)(2,1)} reshape(bf16[128,10,2048]{2,1,0:T(8,128)(2,1)} %all-to-all-done.6) | data formatting | bytes 10485760 | tf_op jit(solution)/shard_map/reshape | solution.py:142
  665.3 12.0 %gather_fusion.4 = bf16[1024,2048]{1,0:T(8,128)(2,1)} fusion(bf16[1280,2048]{1,0:T(8,128)(2,1)} %reshape.191, s32[1024]{0:T(1024)S(1)} %broadcast_clamp_fusion), kind=kCustom, calls=%fused_computation.4 | custom fusion | bytes 8392704 | tf_op jit(solution)/shard_map/gather | solution.py:144
  677.3 8.7 %convert_reduce_fusion = (f32[128,2048]{1,0:T(8,128)S(1)}, f32[128,2048]{1,0:T(8,128)S(1)}) fusion(bf16[1024,2048]{1,0:T(8,128)(2,1)} %gather_fusion.4, f32[128,8]{1,0:T(8,128)S(1)} %copy.42, bf16[1024,2048]{1,0:T(8,128)(2,1)} %gather_fusion.1), kind=kLoop, calls=%fused_computation.13 | loop fusion | flops 9961472 | bytes 10489856 | tf_op jit(solution)/shard_map/reduce_sum | solution.py:143
  (110 shorter events, 71.7 us)
Async XLA Ops:
  7.2 338.6 %copy-start = (bf16[1,768,2048]{2,1,0:T(8,128)(2,1)S(1)}, bf16[1,768,2048]{2,1,0:T(8,128)(2,1)}, u32[]{:S(2)}) copy-start(bf16[1,768,2048]{2,1,0:T(8,128)(2,1)} %param.22) | copy-start | bytes 9437188
  7.2 19.7 %copy-start.9 = (bf16[1,128,512]{2,1,0:T(8,128)(2,1)S(1)}, bf16[1,128,512]{2,1,0:T(8,128)(2,1)}, u32[]{:S(2)}) copy-start(bf16[1,128,512]{2,1,0:T(8,128)(2,1)} %param.14) | copy-start | bytes 393220
  9.1 12.1 %all-to-all-start.2 = ((bf16[128,8,128]{0,2,1:T(8,128)(2,1)}), bf16[128,8,128]{0,2,1:T(8,128)(2,1)S(1)}, u32[]{:S(2)}, u32[]{:S(2)}) async-start(bf16[128,8,128]{0,2,1:T(8,128)(2,1)} %bitcast.101), calls=%async_computation.2 | async-start | bytes 524288 | tf_op jit(solution)/shard_map/all_to_all | solution.py:60
  21.2 19.1 %copy-start.7 = (bf16[128,8,128]{0,2,1:T(8,128)(2,1)}, bf16[128,8,128]{0,2,1:T(8,128)(2,1)S(1)}, u32[]{:S(2)}) copy-start(bf16[128,8,128]{0,2,1:T(8,128)(2,1)S(1)} %all-to-all-done.2) | copy-start | bytes 786436
  21.2 18.4 %all-to-all-start.1 = ((bf16[128,8,512]{0,2,1:T(8,128)(2,1)}), bf16[128,8,512]{0,2,1:T(8,128)(2,1)}, u32[]{:S(2)}, u32[]{:S(2)}) async-start(bf16[128,8,512]{0,2,1:T(8,128)(2,1)} %bitcast.97), calls=%async_computation.1 | async-start | bytes 2097152 | tf_op jit(solution)/shard_map/all_to_all | solution.py:58
  40.4 15.5 %all-to-all-start = ((bf16[128,8,128]{2,0,1:T(8,128)(2,1)}), bf16[128,8,128]{2,0,1:T(8,128)(2,1)S(1)}, u32[]{:S(2)}, u32[]{:S(2)}) async-start(bf16[128,8,128]{2,0,1:T(8,128)(2,1)} %bitcast.100), calls=%async_computation | async-start | bytes 524288 | tf_op jit(solution)/shard_map/all_to_all | solution.py:59
  45.8 119.4 %reduce-scatter.2.cloned.1.call-start = ((), (), s32[]{:S(2)}) async-start(), calls=%async_computation.8 | async-start | bytes 4718592 | tf_op jit(solution)/shard_map/reduce_scatter | solution.py:82
  55.8 4.3 copy-start.2
  60.1 3.7 copy-start.8
  63.8 5.5 copy-start.21
  73.7 93.4 %copy-start.10 = (f32[2048]{0:T(1024)S(1)}, f32[2048]{0:T(1024)}, u32[]{:S(2)}) copy-start(f32[2048]{0:T(1024)} %param.17) | copy-start | bytes 24580
  167.1 14.2 %copy-start.14 = (f32[128]{0:T(128)}, f32[128]{0:T(128)S(1)}, u32[]{:S(2)}) copy-start(f32[128]{0:T(128)S(1)} %fusion.33) | copy-start | bytes 1540
  198.2 9.8 %copy-start.12 = (f32[1,128,8]{1,2,0:T(8,128)S(1)}, f32[1,128,8]{1,2,0:T(8,128)}, u32[]{:S(2)}) copy-start(f32[1,128,8]{1,2,0:T(8,128)} %param.19) | copy-start | bytes 12292
  198.2 115.3 %all-to-all-start.3 = ((bf16[128,10,2048]{2,1,0:T(8,128)(2,1)}), bf16[128,10,2048]{2,1,0:T(8,128)(2,1)}, u32[]{:S(2)}, u32[]{:S(2)}) async-start(bf16[128,10,2048]{2,1,0:T(8,128)(2,1)} %broadcast_select_fusion), calls=%async_computation.4 | async-start | bytes 16777216 | tf_op jit(solution)/shard_map/all_to_all | solution.py:26
  313.4 114.3 %all-to-all-start.5 = ((bf16[128,10,2048]{2,1,0:T(8,128)(2,1)}), bf16[128,10,2048]{2,1,0:T(8,128)(2,1)}, u32[]{:S(2)}, u32[]{:S(2)}) async-start(bf16[128,10,2048]{2,1,0:T(8,128)(2,1)} %select_convert_fusion), calls=%async_computation.6 | async-start | bytes 16777216 | tf_op jit(solution)/shard_map/all_to_all | solution.py:26
  332.3 7.3 %copy-start.5 = (bf16[1280,2048]{1,0:T(8,128)(2,1)S(1)}, bf16[1280,2048]{1,0:T(8,128)(2,1)}, u32[]{:S(2)}) copy-start(bf16[1280,2048]{1,0:T(8,128)(2,1)} %reshape.186) | copy-start | bytes 15728644
  332.3 7.3 %copy-start.19 = (bf16[1,2048,768]{2,1,0:T(8,128)(2,1)S(1)}, bf16[1,2048,768]{2,1,0:T(8,128)(2,1)}, u32[]{:S(2)}) copy-start(bf16[1,2048,768]{2,1,0:T(8,128)(2,1)} %param.21) | copy-start | bytes 9437188
  339.5 4.3 copy-start.22
  343.9 1.9 copy-start.25
  427.8 113.8 %all-to-all-start.4 = ((bf16[128,10,2048]{2,1,0:T(8,128)(2,1)}), bf16[128,10,2048]{2,1,0:T(8,128)(2,1)}, u32[]{:S(2)}, u32[]{:S(2)}) async-start(bf16[128,10,2048]{2,1,0:T(8,128)(2,1)} %reshape.187), calls=%async_computation.5 | async-start | bytes 16777216 | tf_op jit(solution)/shard_map/all_to_all | solution.py:26
  446.1 8.4 %copy-start.18 = (bf16[1,2048,768]{2,1,0:T(8,128)(2,1)S(1)}, bf16[1,2048,768]{2,1,0:T(8,128)(2,1)}, u32[]{:S(2)}) copy-start(bf16[1,2048,768]{2,1,0:T(8,128)(2,1)} %param.20) | copy-start | bytes 9437188
  446.1 8.4 %copy-start.23 = (f32[1280,768]{1,0:T(8,128)S(1)}, f32[1280,768]{1,0:T(8,128)}, u32[]{:S(2)}) copy-start(f32[1280,768]{1,0:T(8,128)} %copy-done.22) | copy-start | bytes 11796484
  446.1 8.4 %copy-start.26 = (f32[1280,768]{1,0:T(8,128)S(1)}, f32[1280,768]{1,0:T(8,128)}, u32[]{:S(2)}) copy-start(f32[1280,768]{1,0:T(8,128)} %copy-done.25) | copy-start | bytes 11796484
  452.5 2.0 copy-start.24
  454.5 8.0 %copy-start.20 = (bf16[1,2048,768]{2,1,0:T(8,128)(2,1)S(1)}, bf16[1,2048,768]{2,1,0:T(8,128)(2,1)}, u32[]{:S(2)}) copy-start(bf16[1,2048,768]{2,1,0:T(8,128)(2,1)} %param.21) | copy-start | bytes 9437188
  541.6 113.8 %all-to-all-start.6 = ((bf16[128,10,2048]{2,1,0:T(8,128)(2,1)}), bf16[128,10,2048]{2,1,0:T(8,128)(2,1)}, u32[]{:S(2)}, u32[]{:S(2)}) async-start(bf16[128,10,2048]{2,1,0:T(8,128)(2,1)} %reshape.190), calls=%async_computation.7 | async-start | bytes 16777216 | tf_op jit(solution)/shard_map/all_to_all | solution.py:26
  677.3 8.7 %copy-start.3 = (bf16[1,128,2048]{2,1,0:T(8,128)(2,1)S(1)}, bf16[1,128,2048]{2,1,0:T(8,128)(2,1)}, u32[]{:S(2)}) copy-start(bf16[1,128,2048]{2,1,0:T(8,128)(2,1)} %param.12) | copy-start | bytes 1572868
  677.3 8.7 %copy-start.4 = (bf16[128,2048]{1,0:T(8,128)(2,1)S(1)}, bf16[128,2048]{1,0:T(8,128)(2,1)}, u32[]{:S(2)}) copy-start(bf16[128,2048]{1,0:T(8,128)(2,1)} %reduce-scatter.2.cloned.1.call-done) | copy-start | bytes 1572868
  677.3 8.7 %copy-start.11 = (f32[2048]{0:T(1024)S(1)}, f32[2048]{0:T(1024)}, u32[]{:S(2)}) copy-start(f32[2048]{0:T(1024)} %param.17) | copy-start | bytes 24580
  677.3 9.0 %copy-start.17 = (f32[128]{0:T(128)S(1)}, f32[128]{0:T(128)}, u32[]{:S(2)}) copy-start(f32[128]{0:T(128)} %copy-done.16) | copy-start | bytes 1540
  677.3 9.1 %copy-start.1 = (bf16[1,128,2048]{2,1,0:T(8,128)(2,1)S(1)}, bf16[1,128,2048]{2,1,0:T(8,128)(2,1)}, u32[]{:S(2)}) copy-start(bf16[1,128,2048]{2,1,0:T(8,128)(2,1)} %param.23) | copy-start | bytes 1572868
  677.3 9.1 %copy-start.15 = (f32[128]{0:T(128)S(1)}, f32[128]{0:T(128)}, u32[]{:S(2)}) copy-start(f32[128]{0:T(128)} %copy-done.14) | copy-start | bytes 1540
  (3 other events, 2.0 us)
Sparse Core Ops, SparseCore 0:
  73.8 91.2 reduce-scatter.1
where the time goes:
time: 706 us; the launch traced here: 695 us
  waiting for transfers between devices  375 us (53%)
  local copies, waits for them, and re-layouts  159 us (23%)
  matrix products  56.4 us (8%)
  starting transfers between devices  53.1 us (8%)
  other arithmetic  37.6 us (5%)
  between operations  14.7 us (2%)
    all_to_all x4, waiting for transfers between devices, to_owners(): lax.all_to_all(buffer, ('cp', 'ep'), split_axis=0, concat_axis=0, tiled=T...  278 us
    reduce_scatter x1, waiting for transfers between devices, on_device(): lax.psum_scatter(jnp.dot(attn_out, out_proj, preferred_element_type=jnp.f...  82.7 us
    all_to_all x4, starting transfers between devices, to_owners(): lax.all_to_all(buffer, ('cp', 'ep'), split_axis=0, concat_axis=0, tiled=T...  35.6 us
    gather x2, local copies, waits for them, and re-layouts, on_device(): normed[slot_token]  21.5 us
  transfers between devices with their start and end apart: 8, of which 7 were waited for; matrix products, arithmetic and copies ran while one was open for 23% of the time, Pallas kernels for 0%

commit v1 on v0

--- a/solution.py
+++ b/solution.py
@@ -1,15 +1,364 @@
+import functools
 import jax
 import jax.numpy as jnp
 from jax import lax
+from jax.experimental import pallas as pl
+from jax.experimental.pallas import tpu as pltpu
 from jax.sharding import PartitionSpec as P
 
+MESH = pl.DeviceIdType.MESH
 QHEADS = 32
 KVHEADS = 4
 HEAD = 128
-TOPK = 8
-
-
 EPSILON = 1e-06
+D = 2048
+CAP = 10
+BLK = 80
+COLS = ((0, 640), (640, 640), (1280, 768))
+ROLES = ((2, 0, 1), (0, 1, 2), (1, 2, 0))
+F32 = jnp.float32
+BF16 = jnp.bfloat16
+
+
+def coords():
+    cp = lax.axis_index("cp")
+    ep = lax.axis_index("ep")
+    x = lax.div(ep, 8) * 2 + lax.rem(cp, 2)
+    y = lax.rem(lax.div(ep, 2), 4)
+    z = lax.div(cp, 2)
+    return (x, y, z), lax.rem(ep, 2)
+
+
+def place(pos, core):
+    x, y, z = pos
+    return (z * 2 + lax.rem(x, 2), lax.div(x, 2) * 8 + y * 2 + core)
+
+
+def turn(v, d):
+    return lax.rem(v + d, 4)
+
+
+def moved(pos, axis, d):
+    return tuple(turn(p, d) if i == axis else p for i, p in enumerate(pos))
+
+
+class Net:
+    def __init__(self, send, recv):
+        self.pos, self.core = coords()
+        self.send, self.recv = send, recv
+        self.count = 0
+        self.open = []
+
+    def peer(self, axis, d):
+        return place(moved(self.pos, axis, d), self.core)
+
+    def mate(self):
+        return place(self.pos, 1 - self.core)
+
+    def copy(self, src, dst, target):
+        n = self.count
+        self.count += 1
+        made = pltpu.make_async_remote_copy(
+            src_ref=src, dst_ref=dst, send_sem=self.send.at[n], recv_sem=self.recv.at[n],
+            device_id=target, device_id_type=MESH)
+        self.open.append(made)
+        return made
+
+    def barrier(self):
+        bar = pltpu.get_barrier_semaphore()
+        targets = [self.peer(a, d) for a in range(3) for d in (1, 2, 3)] + [self.mate()]
+        for t in targets:
+            pl.semaphore_signal(bar, inc=1, device_id=t, device_id_type=MESH)
+        pl.semaphore_wait(bar, len(targets))
+
+    def finish(self):
+        for made in self.open:
+            made.wait_send()
+
+
+def swap_matrix():
+    r = lax.broadcasted_iota(jnp.int32, (320, 320), 0)
+    c = lax.broadcasted_iota(jnp.int32, (320, 320), 1)
+    b, rest = lax.div(r, 80), lax.rem(r, 80)
+    a, w = lax.div(rest, 20), lax.rem(rest, 20)
+    return (c == a * 80 + b * 20 + w).astype(F32).astype(BF16)
+
+
+def ranks_to(ids_ref, gates_ref, out_ref, t):
+    a1, a2, a3 = ROLES[t]
+    q = lax.broadcasted_iota(jnp.int32, (128, 128), 0)
+    digit = {a1: lax.div(q, 32), a2: lax.rem(lax.div(q, 4), 4), a3: lax.rem(q, 4)}
+    core = lax.rem(lax.div(q, 16), 2)
+    e0, e1 = place((digit[0], digit[1], digit[2]), core)
+    expert = e0 * 16 + e1
+    named = jnp.zeros((128, 128), F32)
+    gate = jnp.zeros((128, 128), F32)
+    for j in range(8):
+        hit = ids_ref[j:j + 1, :] == expert
+        named = named + jnp.where(hit, 1.0, 0.0)
+        gate = gate + jnp.where(hit, gates_ref[j:j + 1, :], 0.0)
+    lo = lax.broadcasted_iota(jnp.int32, (128, 128), 0)
+    hi = lax.broadcasted_iota(jnp.int32, (128, 128), 1)
+    upto = (lo <= hi).astype(F32).astype(BF16)
+    seen = jnp.dot(named.astype(BF16), upto, preferred_element_type=F32)
+    rank = jnp.where(named > 0.5, seen - 1.0, -1000.0)
+    out_ref[:, :, 0] = rank.reshape(4, 2, 16, 128)
+    out_ref[:, :, 1] = gate.reshape(4, 2, 16, 128)
+
+
+def build_pick(ranks, core, pick_ref, gate_ref=None):
+    rows = lax.broadcasted_iota(jnp.int32, (BLK, 128), 0).astype(F32)
+
+    def step(e, carry):
+        at = pl.multiple_of(e * BLK, 16)
+        total = jnp.zeros((BLK, 128), F32)
+        for s in range(8):
+            rank = ranks[s // 2, s % 2, core, 0, pl.ds(e, 1), :]
+            hit = rank + float(CAP * s) == rows
+            pick_ref[pl.ds(at, BLK), s * 128:(s + 1) * 128] = jnp.where(hit, 1.0, 0.0).astype(BF16)
+            if gate_ref is not None:
+                gate = ranks[s // 2, s % 2, core, 1, pl.ds(e, 1), :]
+                total = total + jnp.where(hit, gate, 0.0)
+        if gate_ref is not None:
+            gate_ref[pl.ds(at, BLK), :] = jnp.sum(total, axis=1, keepdims=True)
+        return carry
+    lax.fori_loop(0, 16, step, 0)
+
+
+def dispatch_kernel(scaled, x_ref, ids_ref, gates_ref, out_ref, ranks_out, *scratch):
+    (ag0, ag1, ag2, sel0, sel1, sel2, mid0, mid1, mid2, end0, end1, end2,
+     own_ranks, pick, gate, send, recv) = scratch
+    ags, sels, mids, ends = (ag0, ag1, ag2), (sel0, sel1, sel2), (mid0, mid1, mid2), (end0, end1, end2)
+    net = Net(send, recv)
+    pos, core = net.pos, net.core
+    net.barrier()
+    gathers, own, rank_sends, mate_ranks = [], [], [], []
+    for t in range(3):
+        a1 = ROLES[t][0]
+        c0, w = COLS[t]
+        src = x_ref.at[:, c0:c0 + w]
+        slot = pos[a1] * 2 + core
+        cps = [net.copy(src, ags[t].at[slot], net.peer(a1, d)) for d in (1, 2, 3)]
+        mate = net.copy(src, ags[t].at[slot], net.mate())
+        for cp in cps + [mate]:
+            cp.start()
+        gathers.append(cps)
+        own.append(mate)
+    for t in range(3):
+        a1 = ROLES[t][0]
+        c0, w = COLS[t]
+        ags[t][pos[a1] * 2 + core] = x_ref[:, c0:c0 + w]
+        ranks_to(ids_ref, gates_ref, own_ranks.at[t], t)
+        cps = [net.copy(own_ranks.at[t, turn(pos[a1], d)], ranks_out.at[t, pos[a1], core], net.peer(a1, d)) for d in (1, 2, 3)]
+        for cp in cps:
+            cp.start()
+        ranks_out[t, pos[a1], core] = own_ranks[t, pos[a1]]
+        mate = net.copy(own_ranks.at[t, pos[a1], 1 - core], ranks_out.at[t, pos[a1], core, 1 - core], net.mate())
+        mate.start()
+        rank_sends.append(cps)
+        mate_ranks.append([mate])
+    forwards = []
+    for t in range(3):
+        a1 = ROLES[t][0]
+        fw = []
+        for i, d in enumerate((1, 2, 3)):
+            rank_sends[t][i].wait_recv()
+            a = turn(pos[a1], 4 - d)
+            cp = net.copy(ranks_out.at[t, a, core, 1 - core], ranks_out.at[t, a, core, 1 - core], net.mate())
+            cp.start()
+            mate_ranks[t].append(cp)
+    for t in range(3):
+        a1 = ROLES[t][0]
+        fw = []
+        for i, d in enumerate((1, 2, 3)):
+            gathers[t][i].wait_recv()
+            s = turn(pos[a1], 4 - d) * 2 + core
+            cp = net.copy(ags[t].at[s], ags[t].at[s], net.mate())
+            cp.start()
+            fw.append(cp)
+        forwards.append(fw)
+    firsts = []
+    for t in range(3):
+        a1, a2, a3 = ROLES[t]
+        w = COLS[t][1]
+        for cp in mate_ranks[t]:
+            cp.wait_recv()
+        build_pick(ranks_out.at[t], core, pick, gate if scaled else None)
+        own[t].wait_recv()
+        for cp in forwards[t]:
+            cp.wait_recv()
+        base = net.count
+        cps = [net.copy(sels[t].at[d - 1], mids[t].at[pos[a2]], net.peer(a2, d)) for d in (1, 2, 3)]
+
+        def chosen(b):
+            at = pl.multiple_of(b * 320, 16)
+            rows = jnp.dot(pick[pl.ds(at, 320), :], ags[t][...].reshape(1024, w), preferred_element_type=F32)
+            if scaled:
+                rows = rows * gate[pl.ds(at, 320), :]
+            return rows.astype(BF16).reshape(4, BLK, w)
+        for d in (1, 2, 3):
+            sels[t][d - 1] = chosen(turn(pos[a2], d))
+            cps[d - 1].start()
+        mids[t][pos[a2]] = chosen(pos[a2])
+        firsts.append(cps)
+    seconds = []
+    for t in range(3):
+        a1, a2, a3 = ROLES[t]
+        sec = []
+        for i in range(4):
+            a = turn(pos[a2], 4 - i)
+            if i:
+                firsts[t][i - 1].wait_recv()
+            for d in (1, 2, 3):
+                cp = net.copy(mids[t].at[a, turn(pos[a3], d)], ends[t].at[pos[a3], a], net.peer(a3, d))
+                cp.start()
+                sec.append(cp)
+            ends[t][pos[a3], a] = mids[t][a, pos[a3]]
+        seconds.append(sec)
+    swap = swap_matrix()
+    for t in range(3):
+        c0, w = COLS[t]
+        for cp in seconds[t]:
+            cp.wait_recv()
+        for g in range(4):
+            if t == 0:
+                out_ref[g * 320:(g + 1) * 320, c0:c0 + w] = ends[t][g].reshape(320, w)
+            elif t == 1:
+                got = jnp.dot(swap, ends[t][:, g].reshape(320, w), preferred_element_type=F32).astype(BF16)
+                out_ref[g * 320:(g + 1) * 320, c0:c0 + w] = got
+            else:
+                got = jnp.dot(swap, ends[t][g].reshape(320, w), preferred_element_type=F32).astype(BF16)
+                for y in range(4):
+                    out_ref[y * 320 + g * BLK:y * 320 + (g + 1) * BLK, c0:c0 + w] = got[y * BLK:(y + 1) * BLK]
+    net.finish()
+
+
+def vm(*shape, dtype=BF16):
+    return pltpu.VMEM(shape, dtype)
+
+
+def dispatch(x, ids_t, gates_t, scaled, cid):
+    v = pl.BlockSpec(memory_space=pltpu.VMEM)
+    ws = [w for _, w in COLS]
+    return pl.pallas_call(
+        functools.partial(dispatch_kernel, scaled),
+        out_shape=(jax.ShapeDtypeStruct((1280, D), BF16), jax.ShapeDtypeStruct((3, 4, 2, 2, 2, 16, 128), F32)),
+        in_specs=[v] * 3, out_specs=(v, v),
+        scratch_shapes=[vm(8, 128, w) for w in ws] + [vm(3, 4, BLK, w) for w in ws] + [vm(4, 4, BLK, w) for w in ws]
+        + [vm(4, 4, BLK, w) for w in ws] + [vm(3, 4, 2, 2, 16, 128, dtype=F32), vm(1280, 1024), vm(1280, 1, dtype=F32),
+                                            pltpu.SemaphoreType.DMA((120,)), pltpu.SemaphoreType.DMA((120,))],
+        compiler_params=pltpu.CompilerParams(collective_id=cid, has_side_effects=True, vmem_limit_bytes=60 * 2**20),
+    )(x, ids_t, gates_t)
+
+
+def return_kernel(eo_ref, gi_ref, ranks, moe_ref, grad_ref, *scratch):
+    (m0, m1, m2, o0, o1, o2, n0, n1, n2, part0, part1, part2, core0, core1, core2, rs0, rs1, rs2, pick, gate, send, recv, local) = scratch
+    outs, mids, news = (o0, o1, o2), (m0, m1, m2), (n0, n1, n2)
+    parts, cores, rss = (part0, part1, part2), (core0, core1, core2), (rs0, rs1, rs2)
+    net = Net(send, recv)
+    pos, core = net.pos, net.core
+    net.barrier()
+    swap = swap_matrix()
+    srcs = (eo_ref, gi_ref)
+    phase1 = {}
+    for k in range(2):
+        for t in range(3):
+            a1, a2, a3 = ROLES[t]
+            c0, w = COLS[t]
+            o = outs[t].at[k]
+            for g in range(4):
+                if t == 0:
+                    o[g] = srcs[k][g * 320:(g + 1) * 320, c0:c0 + w].reshape(4, BLK, w)
+                elif t == 1:
+                    got = jnp.dot(swap, srcs[k][g * 320:(g + 1) * 320, c0:c0 + w], preferred_element_type=F32).astype(BF16)
+                    o[:, g] = got.reshape(4, BLK, w)
+                else:
+                    rows = jnp.concatenate([srcs[k][y * 320 + g * BLK:y * 320 + (g + 1) * BLK, c0:c0 + w] for y in range(4)], axis=0)
+                    o[g] = jnp.dot(swap, rows, preferred_element_type=F32).astype(BF16).reshape(4, BLK, w)
+            cps = []
+            for d in (1, 2, 3):
+                cp = net.copy(o.at[turn(pos[a3], d)], mids[t].at[k, pos[a3]], net.peer(a3, d))
+                cp.start()
+                cps.append(cp)
+            phase1[k, t] = cps
+    phase2, kept = {}, {}
+    for k in range(2):
+        for t in range(3):
+            a1, a2, a3 = ROLES[t]
+            cps = []
+            kept[k, t] = []
+            for i in range(4):
+                a = turn(pos[a3], 4 - i)
+                if i:
+                    phase1[k, t][i - 1].wait_recv()
+                    here = mids[t].at[k, a]
+                else:
+                    here = outs[t].at[k, a]
+                for d in (1, 2, 3):
+                    cp = net.copy(here.at[turn(pos[a2], d)], news[t].at[k, pos[a2], a], net.peer(a2, d))
+                    cp.start()
+                    cps.append(cp)
+                keep = pltpu.make_async_copy(here.at[pos[a2]], news[t].at[k, pos[a2], a], local.at[k * 12 + t * 4 + i])
+                keep.start()
+                kept[k, t].append(keep)
+            phase2[k, t] = cps
+    phase3 = {}
+    for k in range(2):
+        for t in range(3):
+            a1, a2, a3 = ROLES[t]
+            c0, w = COLS[t]
+            build_pick(ranks.at[t], core, pick, gate)
+            for cp in phase2[k, t]:
+                cp.wait_recv()
+            for keep in kept[k, t]:
+                keep.wait()
+            rows = news[t][k].reshape(1280, w)
+            if k == 0:
+                rows = (rows.astype(F32) * gate[...]).astype(BF16)
+            total = lax.dot_general(pick[...], rows, (((0,), (0,)), ((), ())), preferred_element_type=F32)
+            parts[t][k] = total.astype(BF16).reshape(4, 2, 128, w)
+            cp = net.copy(parts[t].at[k, :, 1 - core], cores[t].at[k], net.mate())
+            cp.start()
+            phase3[k, t] = cp
+    phase4 = {}
+    for k in range(2):
+        for t in range(3):
+            a1 = ROLES[t][0]
+            phase3[k, t].wait_recv()
+            cores[t][k] = (cores[t][k].astype(F32) + parts[t][k, :, core].astype(F32)).astype(BF16)
+            cps = []
+            for d in (1, 2, 3):
+                cp = net.copy(cores[t].at[k, turn(pos[a1], d)], rss[t].at[k, d - 1], net.peer(a1, d))
+                cp.start()
+                cps.append(cp)
+            phase4[k, t] = cps
+    dst = (moe_ref, grad_ref)
+    for k in range(2):
+        for t in range(3):
+            a1 = ROLES[t][0]
+            c0, w = COLS[t]
+            total = cores[t][k, pos[a1]].astype(F32)
+            for i, cp in enumerate(phase4[k, t]):
+                cp.wait_recv()
+                total = total + rss[t][k, i].astype(F32)
+            dst[k][:, c0:c0 + w] = total
+    net.finish()
+
+
+def give_back(eo, gi, ranks, cid):
+    v = pl.BlockSpec(memory_space=pltpu.VMEM)
+    ws = [w for _, w in COLS]
+    shape = jax.ShapeDtypeStruct((128, D), F32)
+    return pl.pallas_call(
+        return_kernel,
+        out_shape=(shape, shape) + tuple(jax.ShapeDtypeStruct((2, 4, 4, BLK, w), BF16) for w in ws),
+        in_specs=[v] * 3, out_specs=(v, v) + (pl.BlockSpec(memory_space=pl.ANY),) * 3,
+        scratch_shapes=[vm(2, 4, 4, BLK, w) for w in ws] + [vm(2, 4, 4, BLK, w) for w in ws]
+        + [vm(2, 4, 2, 128, w) for w in ws] + [vm(2, 4, 128, w) for w in ws] + [vm(2, 3, 128, w) for w in ws]
+        + [vm(1280, 1024), vm(1280, 1, dtype=F32), pltpu.SemaphoreType.DMA((200,)), pltpu.SemaphoreType.DMA((200,)),
+           pltpu.SemaphoreType.DMA((24,))],
+        compiler_params=pltpu.CompilerParams(collective_id=cid, has_side_effects=True, vmem_limit_bytes=63 * 2**20),
+    )(eo, gi, ranks)[:2]
 
 
 def norm_rows(hidden_rows, gain):
@@ -20,11 +369,6 @@
 def silu_parts(gate_pre):
     sigmoid_value = jax.nn.sigmoid(gate_pre)
     return (gate_pre * sigmoid_value, sigmoid_value * (1.0 + gate_pre * (1.0 - sigmoid_value)))
-
-
-def to_owners(buffer):
-    moved = lax.all_to_all(buffer, ("cp", "ep"), split_axis=0, concat_axis=0, tiled=True)
-    return moved
 
 
 def on_device(
@@ -88,27 +432,14 @@
     hidden = resid[0].astype(jnp.float32) + attn_proj
     normed_full, pullback = jax.vjp(lambda hidden_rows: norm_rows(hidden_rows, norm_gain), hidden)
     normed = normed_full.astype(jnp.bfloat16)
-    flat_ids = expert_ids[0].reshape(-1)
-    flat_gates = route_gates[0].reshape(-1)
-    total_rows = flat_ids.shape[0]
-    expert_count = cp_count * ep_count
-    capacity = tok_rows * TOPK * 5 // (4 * expert_count)
-    onehot = (flat_ids[:, None] == jnp.arange(expert_count, dtype=jnp.int32)[None, :]).astype(
-        jnp.int32
-    )
-    ranks = jnp.sum(jnp.cumsum(onehot, axis=0) * onehot, axis=1) - 1
-    slot_index = flat_ids * capacity + ranks
-    slot_source = jnp.full((expert_count * capacity,), total_rows, jnp.int32)
-    slot_source = slot_source.at[slot_index].set(jnp.arange(total_rows, dtype=jnp.int32))
-    filled = slot_source < total_rows
-    slot_clamped = jnp.minimum(slot_source, total_rows - 1)
-    slot_token = slot_clamped // TOPK
-    dispatch = jnp.where(filled[:, None], normed[slot_token], jnp.zeros((), jnp.bfloat16))
-    dispatch = dispatch.reshape(expert_count, capacity, model_width)
+    ids_t = expert_ids[0].T
+    gates_t = route_gates[0].T
     gate_weight = w_gate[0]
     up_weight = w_up[0]
     down_weight = w_down[0]
-    arrived = to_owners(dispatch).reshape(expert_count * capacity, model_width)
+    cot_rows = cotangent[0]
+    grad_arrived, _ = dispatch(cot_rows, ids_t, gates_t, True, 5)
+    arrived, ranks = dispatch(normed, ids_t, gates_t, False, 6)
     gate_pre = jnp.dot(arrived, gate_weight, preferred_element_type=jnp.float32)
     up_pre = jnp.dot(arrived, up_weight, preferred_element_type=jnp.float32)
     silu_value, silu_slope = silu_parts(gate_pre)
@@ -116,16 +447,6 @@
     expert_out = jnp.dot(inner, down_weight, preferred_element_type=jnp.float32).astype(
         jnp.bfloat16
     )
-    returned = to_owners(expert_out.reshape(expert_count, capacity, model_width))
-    returned = returned.reshape(expert_count * capacity, model_width)
-    picked = returned[slot_index].astype(jnp.float32).reshape(tok_rows, TOPK, model_width)
-    moe_sum = jnp.sum(picked * flat_gates.reshape(tok_rows, TOPK, 1), axis=1)
-    layer_out = (hidden + moe_sum).astype(jnp.bfloat16)
-    cot_rows = cotangent[0]
-    grad_slots = flat_gates[slot_clamped][:, None] * cot_rows[slot_token].astype(jnp.float32)
-    grad_slots = jnp.where(filled[:, None], grad_slots, 0.0).astype(jnp.bfloat16)
-    grad_arrived = to_owners(grad_slots.reshape(expert_count, capacity, model_width))
-    grad_arrived = grad_arrived.reshape(expert_count * capacity, model_width)
     contract_last = (((1,), (1,)), ((), ()))
     grad_inner = lax.dot_general(
         grad_arrived, down_weight, contract_last, preferred_element_type=jnp.float32
@@ -138,11 +459,9 @@
     grad_input = grad_input + lax.dot_general(
         grad_up, up_weight, contract_last, preferred_element_type=jnp.float32
     )
-    grad_input = grad_input.astype(jnp.bfloat16).reshape(expert_count, capacity, model_width)
-    grad_back = to_owners(grad_input).reshape(expert_count * capacity, model_width)
-    normed_grad = jnp.sum(
-        grad_back[slot_index].astype(jnp.float32).reshape(tok_rows, TOPK, model_width), axis=1
-    )
+    grad_input = grad_input.astype(jnp.bfloat16)
+    moe_sum, normed_grad = give_back(expert_out, grad_input, ranks, 7)
+    layer_out = (hidden + moe_sum).astype(jnp.bfloat16)
     grad_hidden = cot_rows.astype(jnp.float32) + pullback(normed_grad)[0]
     return (layer_out[None], grad_hidden[None])
 

time: 706 us -> 457 us (0.65)
  the two profiles are of different devices: /device:TPU:40 before, /device:TPU:0 now
where the time goes in v1:
time: 457 us; the launch traced here: 454 us
  Pallas kernels  314 us (69%)
  matrix products  58.8 us (13%)
  waiting for transfers between devices  33.8 us (7%)
  between operations  14.6 us (3%)
  starting transfers between devices  13.3 us (3%)
  other arithmetic  12.4 us (3%)
  local copies, waits for them, and re-layouts  7.25 us (2%)
    pallas_call x2, Pallas kernels, dispatch(): pl.pallas_call(functools.partial(dispatch_kernel, scaled), out_shape=(jax...  188 us
    pallas_call x1, Pallas kernels, give_back(): pl.pallas_call(return_kernel, out_shape=(shape, shape) + tuple((jax.Shape...  126 us
    all_to_all x1, waiting for transfers between devices, on_device(): lax.all_to_all(query[0], 'cp', split_axis=1, concat_axis=0, tiled=True)  14.5 us
    dot_general x1, matrix products, on_device(): lax.dot_general(grad_up, up_weight, contract_last, preferred_element_type...  10.4 us
    reduce_scatter x1, waiting for transfers between devices, on_device(): lax.psum_scatter(jnp.dot(attn_out, out_proj, preferred_element_type=jnp.f...  9.74 us
    dot_general x1, matrix products, on_device(): lax.dot_general(grad_arrived, down_weight, contract_last, preferred_eleme...  9.72 us
  transfers between devices with their start and end apart: 4, of which 4 were waited for; matrix products, arithmetic and copies ran while one was open for 3% of the time, Pallas kernels for 24%

profile of v1, /device:TPU:0, one launch (start us, length us, event | category | flops | bytes accessed | tf_op | source)
XLA Modules:
  0.0 454.2 jit_solution(1300793472651800474)
XLA Ops:
  7.2 1.1 copy.31
  8.2 0.7 broadcast_in_dim.35
  9.0 6.3 %all-to-all-start.2 = ((bf16[128,8,128]{0,2,1:T(8,128)(2,1)}), bf16[128,8,128]{0,2,1:T(8,128)(2,1)S(1)}, u32[]{:S(2)}, u32[]{:S(2)}) async-start(bf16[128,8,128]{0,2,1:T(8,128)(2,1)} %bitcast.11), calls=%async_computation.2 | async-start | bytes 524288 | tf_op jit(solution)/shard_map/all_to_all | solution.py:404
  15.3 2.3 copy.23
  17.6 5.0 %all-to-all-done.2 = bf16[128,8,128]{0,2,1:T(8,128)(2,1)S(1)} async-done(((bf16[128,8,128]{0,2,1:T(8,128)(2,1)}), bf16[128,8,128]{0,2,1:T(8,128)(2,1)S(1)}, u32[]{:S(2)}, u32[]{:S(2)}) %all-to-all-start.2) | async-done | bytes 262176 | tf_op jit(solution)/shard_map/all_to_all | solution.py:404
  22.6 3.6 all-to-all-start.1
  26.2 14.5 %all-to-all-done.1 = bf16[128,8,512]{0,2,1:T(8,128)(2,1)S(1)} async-done(((bf16[128,8,512]{0,2,1:T(8,128)(2,1)}), bf16[128,8,512]{0,2,1:T(8,128)(2,1)S(1)}, u32[]{:S(2)}, u32[]{:S(2)}) %all-to-all-start.1) | async-done | bytes 1048608 | tf_op jit(solution)/shard_map/all_to_all | solution.py:402
  40.7 0.7 broadcast_in_dim.33
  41.5 3.4 all-to-all-start
  44.9 0.3 iota_compare_fusion
  45.4 0.8 reshape.88
  46.3 0.7 copy.24
  46.9 0.7 reshape.83
  47.6 4.5 all-to-all-done
  52.1 3.0 fusion.1
  55.1 3.6 fusion
  58.8 5.5 %fusion.16 = bf16[4,1024,128]{1,2,0:T(8,128)(2,1)S(1)} fusion(bf16[1024,128,1]{0,1,2:T(8,128)(2,1)S(1)} %copy-done.1, f32[4,1024]{1,0:T(4,128)S(1)} %fusion, f32[4,1024]{1,0:T(4,128)S(1)} %get-tuple-element.14, f32[1024,1024,4]{1,0,2:T(8,128)S(1)} %get-tuple-element.15, pred[1024,1024]{0,1:T(8,128)(4,1)S(1)} %iota_compare_fusion), kind=kOutput, calls=%fused_computation.28 | convolution fusion | flops 1095237632 | bytes 19169280 | tf_op jit(solution)/shard_map/agqk,kad->qagd/dot_general | solution.py:422
  64.3 4.4 convolution_convert_fusion.1
  68.7 110.7 %shard_map.132 = (bf16[1280,2048]{1,0:T(8,128)(2,1)}, f32[3,4,2,2,2,16,128]{6,5,4,3,2,1,0:T(8,128)}) custom-call(bf16[128,2048]{1,0:T(8,128)(2,1)} %bitcast.85, s32[8,128]{1,0:T(8,128)} %bitcast.89, f32[8,128]{1,0:T(8,128)} %bitcast.91), custom_call_target="tpu_custom_call" | custom-call | tf_op jit(solution)/shard_map/pallas_call | solution.py:243
  179.5 9.7 %fusion.5 = f32[1280,768]{1,0:T(8,128)} fusion(bf16[1280,2048]{1,0:T(8,128)(2,1)} %get-tuple-element.8, bf16[1,768,2048]{2,1,0:T(8,128)(2,1)} %param.22), kind=kOutput, calls=%fused_computation.16 | convolution fusion | flops 4026531840 | bytes 12320768 | tf_op jit(solution)/shard_map/dot_general | solution.py:451
  189.2 9.7 %reduce-scatter.2.cloned.1.call-done = bf16[128,2048]{1,0:T(8,128)(2,1)} async-done(((bf16[1024,2048]{1,0:T(8,128)(2,1)}), bf16[128,2048]{1,0:T(8,128)(2,1)}) %reduce-scatter.2.cloned.1.call-update) | async-done | bytes 524304 | tf_op jit(solution)/shard_map/reduce_scatter | solution.py:426
  199.0 1.3 multiply_reduce_fusion.1
  200.3 2.0 multiply_convert_fusion.6.x_ref
  202.3 77.4 %shard_map.131 = (bf16[1280,2048]{1,0:T(8,128)(2,1)}, f32[3,4,2,2,2,16,128]{6,5,4,3,2,1,0:T(8,128)}) custom-call(bf16[128,2048]{1,0:T(8,128)(2,1)} %multiply_convert_fusion.6.x_ref, s32[8,128]{1,0:T(8,128)} %bitcast.90, f32[8,128]{1,0:T(8,128)} %bitcast.92), custom_call_target="tpu_custom_call" | custom-call | tf_op jit(solution)/shard_map/pallas_call | solution.py:243
  279.7 7.4 %fusion.13 = f32[1280,768]{1,0:T(8,128)S(1)} fusion(bf16[1280,2048]{1,0:T(8,128)(2,1)} %get-tuple-element.7, bf16[1,2048,768]{2,1,0:T(8,128)(2,1)} %param.20), kind=kOutput, calls=%fused_computation.24 | convolution fusion | flops 4026531840 | bytes 12320768 | tf_op jit(solution)/shard_map/dot_general | solution.py:443
  287.2 4.3 fusion.9
  291.6 6.0 %convolution_convert_fusion.eo_ref = bf16[1280,2048]{1,0:T(8,128)(2,1)} fusion(bf16[1,768,2048]{2,1,0:T(8,128)(2,1)S(1)} %copy-done.5, f32[1280,768]{1,0:T(8,128)S(1)} %fusion.9, f32[1280,768]{1,0:T(8,128)S(1)} %fusion.13), kind=kOutput, calls=%fused_computation.8 | convolution fusion | flops 4035051520 | bytes 16252928 | tf_op jit(solution)/shard_map/dot_general | solution.py:447
  297.6 8.0 %fusion.11 = f32[1280,2048]{1,0:T(8,128)} fusion(bf16[1,2048,768]{2,1,0:T(8,128)(2,1)S(1)} %copy-done.6, f32[1280,768]{1,0:T(8,128)S(1)} %fusion.13, f32[1280,768]{1,0:T(8,128)S(1)} %copy-done.9, f32[1280,768]{1,0:T(8,128)S(1)} %fusion.9), kind=kOutput, calls=%fused_computation.22 | convolution fusion | flops 4036362240 | bytes 25427968 | tf_op jit(solution)/shard_map/dot_general | solution.py:456
  305.6 10.4 %add_convert_fusion.gi_ref = bf16[1280,2048]{1,0:T(8,128)(2,1)} fusion(f32[1280,2048]{1,0:T(8,128)} %fusion.11, bf16[1,2048,768]{2,1,0:T(8,128)(2,1)S(1)} %copy-done.7, f32[1280,768]{1,0:T(8,128)S(1)} %copy-done.9, f32[1280,768]{1,0:T(8,128)} %copy-done.10), kind=kOutput, calls=%fused_computation.5 | convolution fusion | flops 4037672960 | bytes 26738688 | tf_op jit(solution)/shard_map/dot_general | solution.py:459
  316.0 125.9 %shard_map.133 = (f32[128,2048]{1,0:T(8,128)}, f32[128,2048]{1,0:T(8,128)}, bf16[2,4,4,80,640]{4,3,2,1,0:T(8,128)(2,1)}, bf16[2,4,4,80,640]{4,3,2,1,0:T(8,128)(2,1)}, bf16[2,4,4,80,768]{4,3,2,1,0:T(8,128)(2,1)}) custom-call(bf16[1280,2048]{1,0:T(8,128)(2,1)} %convolution_convert_fusion.eo_ref, bf16[1280,2048]{1,0:T(8,128)(2,1)} %add_convert_fusion.gi_ref, ...), custom_call_target="tpu_custom_call" | custom-call | tf_op jit(solution)/shard_map/pallas_call | solution.py:352
  441.9 1.6 multiply_reduce_fusion
  443.6 3.5 fusion.20
  (29 shorter events, 0.4 us)
Async XLA Ops:
  7.2 19.0 %copy-start.2 = (bf16[1,128,512]{2,1,0:T(8,128)(2,1)S(1)}, bf16[1,128,512]{2,1,0:T(8,128)(2,1)}, u32[]{:S(2)}) copy-start(bf16[1,128,512]{2,1,0:T(8,128)(2,1)} %param.14) | copy-start | bytes 393220
  9.0 13.6 %all-to-all-start.2 = ((bf16[128,8,128]{0,2,1:T(8,128)(2,1)}), bf16[128,8,128]{0,2,1:T(8,128)(2,1)S(1)}, u32[]{:S(2)}, u32[]{:S(2)}) async-start(bf16[128,8,128]{0,2,1:T(8,128)(2,1)} %bitcast.11), calls=%async_computation.2 | async-start | bytes 524288 | tf_op jit(solution)/shard_map/all_to_all | solution.py:404
  22.6 18.2 %all-to-all-start.1 = ((bf16[128,8,512]{0,2,1:T(8,128)(2,1)}), bf16[128,8,512]{0,2,1:T(8,128)(2,1)S(1)}, u32[]{:S(2)}, u32[]{:S(2)}) async-start(bf16[128,8,512]{0,2,1:T(8,128)(2,1)} %bitcast.5), calls=%async_computation.1 | async-start | bytes 2097152 | tf_op jit(solution)/shard_map/all_to_all | solution.py:402
  41.5 10.6 %all-to-all-start = ((bf16[128,8,128]{2,0,1:T(8,128)(2,1)}), bf16[128,8,128]{2,0,1:T(8,128)(2,1)S(1)}, u32[]{:S(2)}, u32[]{:S(2)}) async-start(bf16[128,8,128]{2,0,1:T(8,128)(2,1)} %bitcast.1), calls=%async_computation | async-start | bytes 524288 | tf_op jit(solution)/shard_map/all_to_all | solution.py:403
  44.9 154.1 %reduce-scatter.2.cloned.1.call-start = ((), (), s32[]{:S(2)}) async-start(), calls=%async_computation.4 | async-start | bytes 4718592 | tf_op jit(solution)/shard_map/reduce_scatter | solution.py:426
  55.1 3.7 copy-start.1
  58.8 5.5 %copy-start.8 = (bf16[512,2048]{1,0:T(8,128)(2,1)S(1)}, bf16[512,2048]{1,0:T(8,128)(2,1)}, u32[]{:S(2)}) copy-start(bf16[512,2048]{1,0:T(8,128)(2,1)} %param.16) | copy-start | bytes 6291460
  179.5 19.5 %copy-start = (bf16[1,128,2048]{2,1,0:T(8,128)(2,1)S(1)}, bf16[1,128,2048]{2,1,0:T(8,128)(2,1)}, u32[]{:S(2)}) copy-start(bf16[1,128,2048]{2,1,0:T(8,128)(2,1)} %param.12) | copy-start | bytes 1572868
  179.5 20.8 %copy-start.3 = (f32[2048]{0:T(1024)S(1)}, f32[2048]{0:T(1024)}, u32[]{:S(2)}) copy-start(f32[2048]{0:T(1024)} %param.17) | copy-start | bytes 24580
  279.7 7.5 %copy-start.4 = (bf16[1280,2048]{1,0:T(8,128)(2,1)S(1)}, bf16[1280,2048]{1,0:T(8,128)(2,1)}, u32[]{:S(2)}) copy-start(bf16[1280,2048]{1,0:T(8,128)(2,1)} %get-tuple-element.7) | copy-start | bytes 15728644
  279.7 7.5 %copy-start.7 = (bf16[1,2048,768]{2,1,0:T(8,128)(2,1)S(1)}, bf16[1,2048,768]{2,1,0:T(8,128)(2,1)}, u32[]{:S(2)}) copy-start(bf16[1,2048,768]{2,1,0:T(8,128)(2,1)} %param.21) | copy-start | bytes 9437188
  287.2 10.4 %copy-start.10 = (f32[1280,768]{1,0:T(8,128)}, f32[1280,768]{1,0:T(8,128)S(1)}, u32[]{:S(2)}) copy-start(f32[1280,768]{1,0:T(8,128)S(1)} %fusion.13) | copy-start | bytes 11796484
  287.2 4.4 copy-start.5
  291.5 6.0 %copy-start.6 = (bf16[1,2048,768]{2,1,0:T(8,128)(2,1)S(1)}, bf16[1,2048,768]{2,1,0:T(8,128)(2,1)}, u32[]{:S(2)}) copy-start(bf16[1,2048,768]{2,1,0:T(8,128)(2,1)} %param.20) | copy-start | bytes 9437188
  291.6 6.0 %copy-start.9 = (f32[1280,768]{1,0:T(8,128)S(1)}, f32[1280,768]{1,0:T(8,128)}, u32[]{:S(2)}) copy-start(f32[1280,768]{1,0:T(8,128)} %fusion.5) | copy-start | bytes 11796484
Sparse Core Ops, SparseCore 0:
  68.9 130.0 reduce-scatter.1

commit v2 on v1

--- a/solution.py
+++ b/solution.py
@@ -7,11 +7,9 @@
 from jax.sharding import PartitionSpec as P
 
 MESH = pl.DeviceIdType.MESH
-QHEADS = 32
-KVHEADS = 4
+D = 2048
+EPSILON = 1e-06
 HEAD = 128
-EPSILON = 1e-06
-D = 2048
 CAP = 10
 BLK = 80
 COLS = ((0, 640), (640, 640), (1280, 768))
@@ -64,9 +62,9 @@
         self.open.append(made)
         return made
 
-    def barrier(self):
+    def barrier(self, more=()):
         bar = pltpu.get_barrier_semaphore()
-        targets = [self.peer(a, d) for a in range(3) for d in (1, 2, 3)] + [self.mate()]
+        targets = list(more) + [self.peer(a, d) for a in range(3) for d in (1, 2, 3)] + [self.mate()]
         for t in targets:
             pl.semaphore_signal(bar, inc=1, device_id=t, device_id_type=MESH)
         pl.semaphore_wait(bar, len(targets))
@@ -125,111 +123,266 @@
     lax.fori_loop(0, 16, step, 0)
 
 
-def dispatch_kernel(scaled, x_ref, ids_ref, gates_ref, out_ref, ranks_out, *scratch):
-    (ag0, ag1, ag2, sel0, sel1, sel2, mid0, mid1, mid2, end0, end1, end2,
-     own_ranks, pick, gate, send, recv) = scratch
-    ags, sels, mids, ends = (ag0, ag1, ag2), (sel0, sel1, sel2), (mid0, mid1, mid2), (end0, end1, end2)
-    net = Net(send, recv)
-    pos, core = net.pos, net.core
-    net.barrier()
-    gathers, own, rank_sends, mate_ranks = [], [], [], []
-    for t in range(3):
-        a1 = ROLES[t][0]
-        c0, w = COLS[t]
-        src = x_ref.at[:, c0:c0 + w]
-        slot = pos[a1] * 2 + core
-        cps = [net.copy(src, ags[t].at[slot], net.peer(a1, d)) for d in (1, 2, 3)]
-        mate = net.copy(src, ags[t].at[slot], net.mate())
-        for cp in cps + [mate]:
-            cp.start()
-        gathers.append(cps)
-        own.append(mate)
-    for t in range(3):
-        a1 = ROLES[t][0]
-        c0, w = COLS[t]
-        ags[t][pos[a1] * 2 + core] = x_ref[:, c0:c0 + w]
-        ranks_to(ids_ref, gates_ref, own_ranks.at[t], t)
-        cps = [net.copy(own_ranks.at[t, turn(pos[a1], d)], ranks_out.at[t, pos[a1], core], net.peer(a1, d)) for d in (1, 2, 3)]
-        for cp in cps:
-            cp.start()
-        ranks_out[t, pos[a1], core] = own_ranks[t, pos[a1]]
-        mate = net.copy(own_ranks.at[t, pos[a1], 1 - core], ranks_out.at[t, pos[a1], core, 1 - core], net.mate())
-        mate.start()
-        rank_sends.append(cps)
-        mate_ranks.append([mate])
-    forwards = []
-    for t in range(3):
-        a1 = ROLES[t][0]
-        fw = []
-        for i, d in enumerate((1, 2, 3)):
-            rank_sends[t][i].wait_recv()
-            a = turn(pos[a1], 4 - d)
-            cp = net.copy(ranks_out.at[t, a, core, 1 - core], ranks_out.at[t, a, core, 1 - core], net.mate())
-            cp.start()
-            mate_ranks[t].append(cp)
-    for t in range(3):
-        a1 = ROLES[t][0]
-        fw = []
-        for i, d in enumerate((1, 2, 3)):
-            gathers[t][i].wait_recv()
-            s = turn(pos[a1], 4 - d) * 2 + core
-            cp = net.copy(ags[t].at[s], ags[t].at[s], net.mate())
-            cp.start()
-            fw.append(cp)
-        forwards.append(fw)
-    firsts = []
-    for t in range(3):
+class Dispatch:
+    def __init__(self, net, scaled, ags, sels, mids, ends, own_ranks, ranks, pick, gate):
+        self.net, self.scaled = net, scaled
+        self.ags, self.sels, self.mids, self.ends = ags, sels, mids, ends
+        self.own_ranks, self.ranks, self.pick, self.gate = own_ranks, ranks, pick, gate
+        self.gathers, self.own, self.rank_sends, self.mate_ranks = [], [], [], []
+        self.forwards, self.firsts, self.seconds = [], [], []
+
+    def gather(self, x_ref):
+        net, pos, core = self.net, self.net.pos, self.net.core
+        for t in range(3):
+            a1 = ROLES[t][0]
+            c0, w = COLS[t]
+            src = x_ref.at[:, c0:c0 + w]
+            slot = pos[a1] * 2 + core
+            cps = [net.copy(src, self.ags[t].at[slot], net.peer(a1, d)) for d in (1, 2, 3)]
+            mate = net.copy(src, self.ags[t].at[slot], net.mate())
+            for cp in cps + [mate]:
+                cp.start()
+            self.gathers.append(cps)
+            self.own.append(mate)
+        for t in range(3):
+            a1 = ROLES[t][0]
+            c0, w = COLS[t]
+            self.ags[t][pos[a1] * 2 + core] = x_ref[:, c0:c0 + w]
+
+    def send_ranks(self, ids_ref, gates_ref):
+        net, pos, core = self.net, self.net.pos, self.net.core
+        own_ranks, ranks = self.own_ranks, self.ranks
+        for t in range(3):
+            a1 = ROLES[t][0]
+            ranks_to(ids_ref, gates_ref, own_ranks.at[t], t)
+            cps = [net.copy(own_ranks.at[t, turn(pos[a1], d)], ranks.at[t, pos[a1], core], net.peer(a1, d)) for d in (1, 2, 3)]
+            for cp in cps:
+                cp.start()
+            ranks[t, pos[a1], core] = own_ranks[t, pos[a1]]
+            mate = net.copy(own_ranks.at[t, pos[a1], 1 - core], ranks.at[t, pos[a1], core, 1 - core], net.mate())
+            mate.start()
+            self.rank_sends.append(cps)
+            self.mate_ranks.append([mate])
+
+    def forward_ranks(self):
+        net, pos, core, ranks = self.net, self.net.pos, self.net.core, self.ranks
+        for t in range(3):
+            a1 = ROLES[t][0]
+            for i, d in enumerate((1, 2, 3)):
+                self.rank_sends[t][i].wait_recv()
+                a = turn(pos[a1], 4 - d)
+                cp = net.copy(ranks.at[t, a, core, 1 - core], ranks.at[t, a, core, 1 - core], net.mate())
+                cp.start()
+                self.mate_ranks[t].append(cp)
+
+    def wait_ranks(self, t):
+        for cp in self.mate_ranks[t]:
+            cp.wait_recv()
+
+    def forward(self):
+        net, pos, core = self.net, self.net.pos, self.net.core
+        for t in range(3):
+            a1 = ROLES[t][0]
+            fw = []
+            for i, d in enumerate((1, 2, 3)):
+                self.gathers[t][i].wait_recv()
+                s = turn(pos[a1], 4 - d) * 2 + core
+                cp = net.copy(self.ags[t].at[s], self.ags[t].at[s], net.mate())
+                cp.start()
+                fw.append(cp)
+            self.forwards.append(fw)
+
+    def select(self, t):
+        net, pos, core = self.net, self.net.pos, self.net.core
         a1, a2, a3 = ROLES[t]
         w = COLS[t][1]
-        for cp in mate_ranks[t]:
+        build_pick(self.ranks.at[t], core, self.pick, self.gate if self.scaled else None)
+        self.own[t].wait_recv()
+        for cp in self.forwards[t]:
             cp.wait_recv()
-        build_pick(ranks_out.at[t], core, pick, gate if scaled else None)
-        own[t].wait_recv()
-        for cp in forwards[t]:
-            cp.wait_recv()
-        base = net.count
-        cps = [net.copy(sels[t].at[d - 1], mids[t].at[pos[a2]], net.peer(a2, d)) for d in (1, 2, 3)]
+        sel, mid = self.sels[t], self.mids[t]
+        cps = [net.copy(sel.at[d - 1], mid.at[pos[a2]], net.peer(a2, d)) for d in (1, 2, 3)]
 
         def chosen(b):
             at = pl.multiple_of(b * 320, 16)
-            rows = jnp.dot(pick[pl.ds(at, 320), :], ags[t][...].reshape(1024, w), preferred_element_type=F32)
-            if scaled:
-                rows = rows * gate[pl.ds(at, 320), :]
+            rows = jnp.dot(self.pick[pl.ds(at, 320), :], self.ags[t][...].reshape(1024, w), preferred_element_type=F32)
+            if self.scaled:
+                rows = rows * self.gate[pl.ds(at, 320), :]
             return rows.astype(BF16).reshape(4, BLK, w)
         for d in (1, 2, 3):
-            sels[t][d - 1] = chosen(turn(pos[a2], d))
+            sel[d - 1] = chosen(turn(pos[a2], d))
             cps[d - 1].start()
-        mids[t][pos[a2]] = chosen(pos[a2])
-        firsts.append(cps)
-    seconds = []
-    for t in range(3):
+        mid[pos[a2]] = chosen(pos[a2])
+        self.firsts.append(cps)
+
+    def second(self, t):
+        net, pos = self.net, self.net.pos
         a1, a2, a3 = ROLES[t]
+        mid, end = self.mids[t], self.ends[t]
         sec = []
         for i in range(4):
             a = turn(pos[a2], 4 - i)
             if i:
-                firsts[t][i - 1].wait_recv()
+                self.firsts[t][i - 1].wait_recv()
             for d in (1, 2, 3):
-                cp = net.copy(mids[t].at[a, turn(pos[a3], d)], ends[t].at[pos[a3], a], net.peer(a3, d))
+                cp = net.copy(mid.at[a, turn(pos[a3], d)], end.at[pos[a3], a], net.peer(a3, d))
                 cp.start()
                 sec.append(cp)
-            ends[t][pos[a3], a] = mids[t][a, pos[a3]]
-        seconds.append(sec)
-    swap = swap_matrix()
-    for t in range(3):
+            end[pos[a3], a] = mid[a, pos[a3]]
+        self.seconds.append(sec)
+
+    def arrive(self, t, out_ref, swap):
         c0, w = COLS[t]
-        for cp in seconds[t]:
+        end = self.ends[t]
+        for cp in self.seconds[t]:
             cp.wait_recv()
         for g in range(4):
             if t == 0:
-                out_ref[g * 320:(g + 1) * 320, c0:c0 + w] = ends[t][g].reshape(320, w)
+                out_ref[g * 320:(g + 1) * 320, c0:c0 + w] = end[g].reshape(320, w)
             elif t == 1:
-                got = jnp.dot(swap, ends[t][:, g].reshape(320, w), preferred_element_type=F32).astype(BF16)
+                got = jnp.dot(swap, end[:, g].reshape(320, w), preferred_element_type=F32).astype(BF16)
                 out_ref[g * 320:(g + 1) * 320, c0:c0 + w] = got
             else:
-                got = jnp.dot(swap, ends[t][g].reshape(320, w), preferred_element_type=F32).astype(BF16)
+                got = jnp.dot(swap, end[g].reshape(320, w), preferred_element_type=F32).astype(BF16)
                 for y in range(4):
                     out_ref[y * 320 + g * BLK:y * 320 + (g + 1) * BLK, c0:c0 + w] = got[y * BLK:(y + 1) * BLK]
+
+
+def dispatch_kernel(scaled, x_ref, ids_ref, gates_ref, out_ref, ranks_out, *scratch):
+    (ag0, ag1, ag2, sel0, sel1, sel2, mid0, mid1, mid2, end0, end1, end2,
+     own_ranks, pick, gate, send, recv) = scratch
+    net = Net(send, recv)
+    net.barrier()
+    work = Dispatch(net, scaled, (ag0, ag1, ag2), (sel0, sel1, sel2), (mid0, mid1, mid2), (end0, end1, end2),
+                    own_ranks, ranks_out, pick, gate)
+    work.gather(x_ref)
+    work.send_ranks(ids_ref, gates_ref)
+    work.forward_ranks()
+    work.forward()
+    for t in range(3):
+        work.wait_ranks(t)
+        work.select(t)
+    for t in range(3):
+        work.second(t)
+    swap = swap_matrix()
+    for t in range(3):
+        work.arrive(t, out_ref, swap)
+    net.finish()
+
+
+def front_kernel(q_ref, k_ref, v_ref, w_ref, resid_ref, gain_ref, cot_ref, ids_ref, gates_ref,
+                 hidden_ref, normed_ref, out_ref, ranks_out, *scratch):
+    (ag0, ag1, ag2, sel0, sel1, sel2, mid0, mid1, mid2, end0, end1, end2,
+     own_ranks, pick, gate, qbuf, kbuf, vbuf, wbuf, att, part, rs, send, recv, local) = scratch
+    net = Net(send, recv)
+    pos, core = net.pos, net.core
+    x, y, z = pos
+    side = lax.rem(x, 2)
+    other = x + 1 - 2 * side
+    net.barrier([place((other, y, turn(z, d)), core) for d in (1, 2, 3)])
+    work = Dispatch(net, True, (ag0, ag1, ag2), (sel0, sel1, sel2), (mid0, mid1, mid2), (end0, end1, end2),
+                    own_ranks, ranks_out, pick, gate)
+    block = z * 2 + side
+
+    def heads(ref, group, width):
+        return ref.at[:, pl.ds(pl.multiple_of(group * width, width), width)]
+    moves = []
+    for d in (1, 2, 3):
+        g = turn(z, d)
+        moves.append(net.copy(heads(q_ref, g, 1024), qbuf.at[z], net.peer(2, d)))
+    for d in (1, 2, 3, 0):
+        g = turn(z, d)
+        for xx in (x, other):
+            if d or xx is other:
+                for ref, buf in ((k_ref, kbuf), (v_ref, vbuf)):
+                    moves.append(net.copy(heads(ref, g, 128), buf.at[block], place((xx, y, g), core)))
+    for cp in moves:
+        cp.start()
+    keeps = [pltpu.make_async_copy(heads(q_ref, z, 1024), qbuf.at[z], local.at[0]),
+             pltpu.make_async_copy(heads(k_ref, z, 128), kbuf.at[block], local.at[1]),
+             pltpu.make_async_copy(heads(v_ref, z, 128), vbuf.at[block], local.at[2]),
+             pltpu.make_async_copy(w_ref, wbuf.at[side], local.at[3])]
+    for cp in keeps:
+        cp.start()
+    work.gather(cot_ref)
+    work.send_ranks(ids_ref, gates_ref)
+    quarters = []
+    for i, d in enumerate((1, 3)):
+        at = pl.ds(pl.multiple_of((core * 2 + i) * 128, 128), 128)
+        cp = net.copy(w_ref.at[at], wbuf.at[side, at], net.peer(0, d))
+        cp.start()
+        quarters.append(cp)
+    work.forward_ranks()
+    work.forward()
+    for t in range(3):
+        work.wait_ranks(t)
+        work.select(t)
+    for cp in quarters:
+        cp.wait_recv()
+    at = pl.ds(pl.multiple_of(core * 256, 256), 256)
+    half = net.copy(wbuf.at[1 - side, at], wbuf.at[1 - side, at], net.mate())
+    half.start()
+    for cp in moves:
+        cp.wait_recv()
+    for cp in keeps:
+        cp.wait()
+    sends = []
+    for zp in (3, 2, 1, 0):
+        span = 256 * (zp + 1)
+
+        def pair(i, carry):
+            lanes = pl.multiple_of(i * 256, 256)
+            two = qbuf[zp, :, pl.ds(lanes, 256)]
+            rows = jnp.concatenate([two[:, :128], two[:, 128:]], axis=0)
+            scores = lax.dot_general(rows, kbuf[0:2 * zp + 2].reshape(span, 128), (((1,), (1,)), ((), ())),
+                                     preferred_element_type=F32) * HEAD ** (-0.5)
+            row = lax.broadcasted_iota(jnp.int32, (256, span), 0)
+            col = lax.broadcasted_iota(jnp.int32, (256, span), 1)
+            seen = col <= lax.rem(row, 128) + (2 * zp + side) * 128
+            scores = jnp.where(seen, scores, -jnp.inf)
+            weights = jnp.exp(scores - jnp.max(scores, axis=1, keepdims=True))
+            probs = (weights / jnp.sum(weights, axis=1, keepdims=True)).astype(BF16)
+            got = jnp.dot(probs, vbuf[0:2 * zp + 2].reshape(span, 128), preferred_element_type=F32).astype(BF16)
+            att[zp, :, pl.ds(lanes, 256)] = jnp.concatenate([got[:128], got[128:]], axis=1)
+            return carry
+        lax.fori_loop(0, 4, pair, 0)
+        if zp == 3:
+            half.wait_recv()
+
+        def project(i, carry):
+            lanes = pl.ds(pl.multiple_of(i * 512, 512), 512)
+            total = jnp.dot(att[zp], wbuf[:, :, lanes].reshape(1024, 512), preferred_element_type=F32)
+            part[zp, :, lanes] = total.astype(BF16)
+            return carry
+        lax.fori_loop(0, 4, project, 0)
+        far = lax.rem(zp + 4 - z, 4)
+        slot = lax.rem(far + 3, 4)
+        cp = pltpu.make_async_remote_copy(
+            src_ref=part.at[zp], dst_ref=rs.at[slot], send_sem=local.at[4 + zp], recv_sem=local.at[8 + slot],
+            device_id=place((x, y, zp), core), device_id_type=MESH)
+
+        @pl.when(zp != z)
+        def _():
+            cp.start()
+        sends.append(cp)
+    for t in range(3):
+        work.second(t)
+    total = resid_ref[...].astype(F32) + part[z].astype(F32)
+    for d in (1, 2, 3):
+        pltpu.make_async_remote_copy(
+            src_ref=part.at[0], dst_ref=rs.at[d - 1], send_sem=local.at[4], recv_sem=local.at[7 + d],
+            device_id=net.peer(2, d), device_id_type=MESH).wait_recv()
+        total = total + rs[d - 1].astype(F32)
+    hidden_ref[...] = total
+    scale = lax.rsqrt(jnp.mean(total * total, axis=1, keepdims=True) + EPSILON)
+    normed_ref[...] = (total * scale * gain_ref[...]).astype(BF16)
+    swap = swap_matrix()
+    for t in range(3):
+        work.arrive(t, out_ref, swap)
+    for zp in range(4):
+        @pl.when(zp != z)
+        def _():
+            sends[3 - zp].wait_send()
     net.finish()
 
 
@@ -249,6 +402,22 @@
                                             pltpu.SemaphoreType.DMA((120,)), pltpu.SemaphoreType.DMA((120,))],
         compiler_params=pltpu.CompilerParams(collective_id=cid, has_side_effects=True, vmem_limit_bytes=60 * 2**20),
     )(x, ids_t, gates_t)
+
+
+def front(q, k, v, w, resid, gain, cot, ids_t, gates_t, cid):
+    vs = pl.BlockSpec(memory_space=pltpu.VMEM)
+    ws = [width for _, width in COLS]
+    return pl.pallas_call(
+        front_kernel,
+        out_shape=(jax.ShapeDtypeStruct((128, D), F32), jax.ShapeDtypeStruct((128, D), BF16),
+                   jax.ShapeDtypeStruct((1280, D), BF16), jax.ShapeDtypeStruct((3, 4, 2, 2, 2, 16, 128), F32)),
+        in_specs=[vs] * 9, out_specs=(vs,) * 4,
+        scratch_shapes=[vm(8, 128, w) for w in ws] + [vm(3, 4, BLK, w) for w in ws] + [vm(4, 4, BLK, w) for w in ws]
+        + [vm(4, 4, BLK, w) for w in ws] + [vm(3, 4, 2, 2, 16, 128, dtype=F32), vm(1280, 1024), vm(1280, 1, dtype=F32),
+           vm(4, 128, 1024), vm(8, 128, 128), vm(8, 128, 128), vm(2, 512, D), vm(4, 128, 1024), vm(4, 128, D), vm(3, 128, D),
+           pltpu.SemaphoreType.DMA((150,)), pltpu.SemaphoreType.DMA((150,)), pltpu.SemaphoreType.DMA((11,))],
+        compiler_params=pltpu.CompilerParams(collective_id=cid, has_side_effects=True, vmem_limit_bytes=62 * 2**20),
+    )(q, k, v, w, resid, gain, cot, ids_t, gates_t)
 
 
 def return_kernel(eo_ref, gi_ref, ranks, moe_ref, grad_ref, *scratch):
@@ -385,60 +554,14 @@
     w_down,
     cotangent,
 ):
-    cp_count = lax.axis_size("cp")
-    ep_count = lax.axis_size("ep")
-    tok_rows = resid.shape[1]
-    model_width = resid.shape[2]
-    seq_rows = tok_rows * cp_count
-    kv_repeat = max(cp_count // KVHEADS, 1)
-
-    def widen(source):
-        split_heads = source[0].reshape(tok_rows, KVHEADS, HEAD)
-        return jnp.repeat(split_heads, kv_repeat, axis=1).reshape(
-            tok_rows, KVHEADS * kv_repeat * HEAD
-        )
-
-    head_query, head_keys, head_values = (
-        lax.all_to_all(query[0], "cp", split_axis=1, concat_axis=0, tiled=True),
-        lax.all_to_all(widen(keys), "cp", split_axis=1, concat_axis=0, tiled=True),
-        lax.all_to_all(widen(values), "cp", split_axis=1, concat_axis=0, tiled=True),
-    )
-    local_heads = QHEADS // cp_count
-    local_kv = KVHEADS * kv_repeat // cp_count
-    per_group = local_heads // local_kv
-    grouped_query = head_query.reshape(seq_rows, local_kv, per_group, HEAD)
-    grouped_keys = head_keys.reshape(seq_rows, local_kv, HEAD)
-    grouped_values = head_values.reshape(seq_rows, local_kv, HEAD)
-    scores = jnp.einsum(
-        "qagd,kad->agqk", grouped_query, grouped_keys, preferred_element_type=jnp.float32
-    ) * HEAD ** (-0.5)
-    causal = lax.broadcasted_iota(jnp.int32, (seq_rows, seq_rows), 0) >= lax.broadcasted_iota(
-        jnp.int32, (seq_rows, seq_rows), 1
-    )
-    scores = jnp.where(causal[None, None], scores, -jnp.inf)
-    highest = jnp.max(scores, axis=-1, keepdims=True)
-    weights = jnp.exp(scores - highest)
-    probs = (weights / jnp.sum(weights, axis=-1, keepdims=True)).astype(jnp.bfloat16)
-    attended = jnp.einsum(
-        "agqk,kad->qagd", probs, grouped_values, preferred_element_type=jnp.float32
-    )
-    attn_out = attended.reshape(seq_rows, local_heads * HEAD).astype(jnp.bfloat16)
-    attn_proj = lax.psum_scatter(
-        jnp.dot(attn_out, out_proj, preferred_element_type=jnp.float32).astype(jnp.bfloat16),
-        "cp",
-        scatter_dimension=0,
-        tiled=True,
-    ).astype(jnp.float32)
-    hidden = resid[0].astype(jnp.float32) + attn_proj
-    normed_full, pullback = jax.vjp(lambda hidden_rows: norm_rows(hidden_rows, norm_gain), hidden)
-    normed = normed_full.astype(jnp.bfloat16)
     ids_t = expert_ids[0].T
     gates_t = route_gates[0].T
     gate_weight = w_gate[0]
     up_weight = w_up[0]
     down_weight = w_down[0]
     cot_rows = cotangent[0]
-    grad_arrived, _ = dispatch(cot_rows, ids_t, gates_t, True, 5)
+    hidden, normed, grad_arrived, _ = front(query[0], keys[0], values[0], out_proj, resid[0], norm_gain[None], cot_rows, ids_t, gates_t, 5)
+    _, pullback = jax.vjp(lambda hidden_rows: norm_rows(hidden_rows, norm_gain), hidden)
     arrived, ranks = dispatch(normed, ids_t, gates_t, False, 6)
     gate_pre = jnp.dot(arrived, gate_weight, preferred_element_type=jnp.float32)
     up_pre = jnp.dot(arrived, up_weight, preferred_element_type=jnp.float32)

time: 457 us -> 385 us (0.84)
  waiting for transfers between devices: 33.8 us -> 0 us
  matrix products: 58.8 us -> 43 us
  between operations: 14.6 us -> 1.26 us
  starting transfers between devices: 13.3 us -> 0 us
  Pallas kernels: 314 us -> 326 us
  other arithmetic: 12.4 us -> 5.15 us
  local copies, waits for them, and re-layouts: 7.25 us -> 1.98 us
    pallas_call x0 -> x1, Pallas kernels: none -> 123 us  [front(): pl.pallas_call(front_kernel, out_shape=(jax.ShapeDtypeStruct((128, D), F3...]
    pallas_call x2 -> x1, Pallas kernels: 188 us -> 76.5 us  [dispatch(): pl.pallas_call(functools.partial(dispatch_kernel, scaled), out_shape=(jax...]
    all_to_all x3 -> x0, waiting for transfers between devices: 24 us -> none  [the longest x1 14.5 us: on_device(): lax.all_to_all(query[0], 'cp', split_axis=1, concat_axis=0, tiled=True)]
    all_to_all x3 -> x0, starting transfers between devices: 13.3 us -> none  [the longest x1 6.32 us: on_device(): lax.all_to_all(widen(values), 'cp', split_axis=1, concat_axis=0, tiled=True)]
    dot_general x3 -> x0, matrix products: 12.9 us -> none  [the longest x1 5.46 us: on_device(): jnp.einsum('agqk,kad->qagd', probs, grouped_values, preferred_element_typ...]
    reduce_scatter x1 -> x0, waiting for transfers between devices: 9.74 us -> none  [on_device(): lax.psum_scatter(jnp.dot(attn_out, out_proj, preferred_element_type=jnp.f...]
    dot_general x1, matrix products: 9.72 us -> 4.33 us  [on_device(): lax.dot_general(grad_arrived, down_weight, contract_last, preferred_eleme...]
    reduce_sum x2 -> x0, other arithmetic: 5.29 us -> none  [the longest x1 3.65 us: on_device(): jnp.sum(weights, axis=-1, keepdims=True)]
  transfers between devices with their start and end apart: 4 -> 0, of which waited for: 4 -> 0; matrix products, arithmetic and copies ran while one was open for 3% -> 0% of each run, Pallas kernels for 24% -> 0%
where the time goes in v2:
time: 385 us; the launch traced here: 378 us
  Pallas kernels  326 us (85%)
  matrix products  43 us (11%)
  other arithmetic  5.15 us (1%)
    pallas_call x1, Pallas kernels, give_back(): pl.pallas_call(return_kernel, out_shape=(shape, shape) + tuple((jax.Shape...  127 us
    pallas_call x1, Pallas kernels, front(): pl.pallas_call(front_kernel, out_shape=(jax.ShapeDtypeStruct((128, D), F3...  123 us
    pallas_call x1, Pallas kernels, dispatch(): pl.pallas_call(functools.partial(dispatch_kernel, scaled), out_shape=(jax...  76.5 us
    dot_general x1, matrix products, on_device(): lax.dot_general(grad_up, up_weight, contract_last, preferred_element_type...  10.2 us
    dot_general x1, matrix products, on_device(): jnp.dot(inner, down_weight, preferred_element_type=jnp.float32)  8.66 us
    dot_general x1, matrix products, on_device(): lax.dot_general(grad_gate, gate_weight, contract_last, preferred_element_...  8.08 us

profile of v2, /device:TPU:0, one launch (start us, length us, event | category | flops | bytes accessed | tf_op | source)
XLA Modules:
  0.0 377.8 jit_solution(13933385461960334775)
XLA Ops:
  0.6 122.7 %shard_map.131 = (f32[128,2048]{1,0:T(8,128)}, bf16[128,2048]{1,0:T(8,128)(2,1)}, bf16[1280,2048]{1,0:T(8,128)(2,1)}, f32[3,4,2,2,2,16,128]{6,5,4,3,2,1,0:T(8,128)}) custom-call(bf16[128,4096]{1,0:T(8,128)(2,1)} %bitcast.36, bf16[128,512]{1,0:T(8,128)(2,1)} %bitcast.38, bf16[128,512]{1,0:T(8,128)(2,1)} %bitcast.39, bf16[512,2048]{1,0:T(8,128)(2,1)} %w_ref.1, ...), custom_call_target="tpu_custom_call" | custom-call | tf_op jit(solution)/shard_map/pallas_call | solution.py:410
  123.4 76.5 %shard_map.132 = (bf16[1280,2048]{1,0:T(8,128)(2,1)}, f32[3,4,2,2,2,16,128]{6,5,4,3,2,1,0:T(8,128)}) custom-call(bf16[128,2048]{1,0:T(8,128)(2,1)} %get-tuple-element.10.x_ref, s32[8,128]{1,0:T(8,128)} %bitcast.42, f32[8,128]{1,0:T(8,128)} %bitcast.44), custom_call_target="tpu_custom_call" | custom-call | tf_op jit(solution)/shard_map/pallas_call | solution.py:396
  199.9 0.0 copy-start.2
  199.9 0.0 copy-start.4
  199.9 0.0 slice-start
  199.9 7.4 %fusion.9 = f32[1280,768]{1,0:T(8,128)S(1)} fusion(bf16[1280,2048]{1,0:T(8,128)(2,1)} %get-tuple-element.11, bf16[1,2048,768]{2,1,0:T(8,128)(2,1)} %param.20), kind=kOutput, calls=%fused_computation.15 | convolution fusion | flops 4026531840 | bytes 12320768 | tf_op jit(solution)/shard_map/dot_general | solution.py:566
  207.3 0.0 copy-done.2
  207.3 0.0 copy-done.4
  207.3 0.0 slice-start.1
  207.4 0.0 copy-start.5
  207.4 4.3 %fusion.5 = f32[1280,768]{1,0:T(8,128)S(1)} fusion(bf16[1280,2048]{1,0:T(8,128)(2,1)S(1)} %copy-done.2, bf16[1,2048,768]{2,1,0:T(8,128)(2,1)S(1)} %copy-done.4), kind=kOutput, calls=%fused_computation.11 | convolution fusion | flops 4026531840 | bytes 12320768 | tf_op jit(solution)/shard_map/dot_general | solution.py:567
  211.7 0.0 copy-start.7
  211.7 0.0 slice-done
  211.7 0.0 slice-done.1
  211.7 0.0 copy-done.5
  211.7 0.0 copy-start.3
  211.8 4.3 %fusion.1 = f32[1280,768]{1,0:T(8,128)S(1)} fusion(bf16[1280,2048]{1,0:T(8,128)(2,1)S(1)} %bitcast.46, bf16[1,768,2048]{2,1,0:T(8,128)(2,1)S(1)} %copy-done.5), kind=kOutput, calls=%fused_computation.7 | convolution fusion | flops 4026531840 | bytes 12320768 | tf_op jit(solution)/shard_map/dot_general | solution.py:574
  216.1 0.0 copy-done.7
  216.1 0.0 copy-start.6
  216.1 1.9 copy-done.6
  218.0 0.0 copy-done.3
  218.0 8.1 %fusion.7 = f32[1280,2048]{1,0:T(8,128)} fusion(bf16[1,2048,768]{2,1,0:T(8,128)(2,1)S(1)} %copy-done.3, f32[1280,768]{1,0:T(8,128)S(1)} %fusion.9, f32[1280,768]{1,0:T(8,128)S(1)} %fusion.1, f32[1280,768]{1,0:T(8,128)S(1)} %fusion.5), kind=kOutput, calls=%fused_computation.13 | convolution fusion | flops 4036362240 | bytes 25427968 | tf_op jit(solution)/shard_map/dot_general | solution.py:579
  226.1 10.2 %add_convert_fusion.gi_ref = bf16[1280,2048]{1,0:T(8,128)(2,1)} fusion(f32[1280,2048]{1,0:T(8,128)} %fusion.7, bf16[1,2048,768]{2,1,0:T(8,128)(2,1)S(1)} %copy-done.4, f32[1280,768]{1,0:T(8,128)} %copy-done.6, f32[1280,768]{1,0:T(8,128)S(1)} %fusion.9), kind=kOutput, calls=%fused_computation | convolution fusion | flops 4037672960 | bytes 26738688 | tf_op jit(solution)/shard_map/dot_general | solution.py:582
  236.3 8.7 %convolution_convert_fusion.eo_ref = bf16[1280,2048]{1,0:T(8,128)(2,1)} fusion(bf16[1,768,2048]{2,1,0:T(8,128)(2,1)S(1)} %copy-done.5, f32[1280,768]{1,0:T(8,128)} %copy-done.7, f32[1280,768]{1,0:T(8,128)S(1)} %fusion.9), kind=kOutput, calls=%fused_computation.1 | convolution fusion | flops 4035051520 | bytes 16252928 | tf_op jit(solution)/shard_map/dot_general | solution.py:570
  245.0 0.0 copy-start.1
  245.0 0.0 copy-start
  245.0 127.2 %shard_map.133 = (f32[128,2048]{1,0:T(8,128)}, f32[128,2048]{1,0:T(8,128)}, bf16[2,4,4,80,640]{4,3,2,1,0:T(8,128)(2,1)}, bf16[2,4,4,80,640]{4,3,2,1,0:T(8,128)(2,1)}, bf16[2,4,4,80,768]{4,3,2,1,0:T(8,128)(2,1)}) custom-call(bf16[1280,2048]{1,0:T(8,128)(2,1)} %convolution_convert_fusion.eo_ref, bf16[1280,2048]{1,0:T(8,128)(2,1)} %add_convert_fusion.gi_ref, ...), custom_call_target="tpu_custom_call" | custom-call | tf_op jit(solution)/shard_map/pallas_call | solution.py:521
  372.2 0.0 copy-done.1
  372.2 1.8 multiply_reduce_fusion.1
  374.0 0.0 copy-done
  374.0 3.3 fusion.13
  (2 shorter events, 0.0 us)
Async XLA Ops:
  199.9 7.5 %copy-start.2 = (bf16[1280,2048]{1,0:T(8,128)(2,1)S(1)}, bf16[1280,2048]{1,0:T(8,128)(2,1)}, u32[]{:S(2)}) copy-start(bf16[1280,2048]{1,0:T(8,128)(2,1)} %get-tuple-element.11) | copy-start | bytes 15728644
  199.9 7.5 %copy-start.4 = (bf16[1,2048,768]{2,1,0:T(8,128)(2,1)S(1)}, bf16[1,2048,768]{2,1,0:T(8,128)(2,1)}, u32[]{:S(2)}) copy-start(bf16[1,2048,768]{2,1,0:T(8,128)(2,1)} %param.21) | copy-start | bytes 9437188
  199.9 11.8 %slice-start = ((s8[5242880]{0:T(1024)(128)(4,1)}), s8[4194304]{0:T(1024)(128)(4,1)S(1)}, s32[]{:S(2)}) async-start(s8[5242880]{0:T(1024)(128)(4,1)} %bitcast.45), calls=%async_computation | async-start | bytes 8388608
  207.3 4.4 %slice-start.1 = ((s8[5242880]{0:T(1024)(128)(4,1)}), s8[1048576]{0:T(1024)(128)(4,1)S(1)}, s32[]{:S(2)}) async-start(s8[5242880]{0:T(1024)(128)(4,1)} %bitcast.45), calls=%async_computation.1 | async-start | bytes 2097152
  207.4 4.4 %copy-start.5 = (bf16[1,768,2048]{2,1,0:T(8,128)(2,1)S(1)}, bf16[1,768,2048]{2,1,0:T(8,128)(2,1)}, u32[]{:S(2)}) copy-start(bf16[1,768,2048]{2,1,0:T(8,128)(2,1)} %param.22) | copy-start | bytes 9437188
  211.7 4.4 %copy-start.7 = (f32[1280,768]{1,0:T(8,128)}, f32[1280,768]{1,0:T(8,128)S(1)}, u32[]{:S(2)}) copy-start(f32[1280,768]{1,0:T(8,128)S(1)} %fusion.5) | copy-start | bytes 11796484
  211.7 6.3 %copy-start.3 = (bf16[1,2048,768]{2,1,0:T(8,128)(2,1)S(1)}, bf16[1,2048,768]{2,1,0:T(8,128)(2,1)}, u32[]{:S(2)}) copy-start(bf16[1,2048,768]{2,1,0:T(8,128)(2,1)} %param.20) | copy-start | bytes 9437188
  216.1 1.9 copy-start.6
  245.0 127.2 %copy-start.1 = (f32[2048]{0:T(1024)S(1)}, f32[2048]{0:T(1024)}, u32[]{:S(2)}) copy-start(f32[2048]{0:T(1024)} %param.17) | copy-start | bytes 24580
  245.0 129.0 %copy-start = (bf16[1,128,2048]{2,1,0:T(8,128)(2,1)S(1)}, bf16[1,128,2048]{2,1,0:T(8,128)(2,1)}, u32[]{:S(2)}) copy-start(bf16[1,128,2048]{2,1,0:T(8,128)(2,1)} %param.23) | copy-start | bytes 1572868
